TPU v7x, 32 devices: a whole 2x2x4 slice. The times are simulated.
32 devices in a mesh: batch: 8 (over y, x, core), head: 4 (over z).
Axes of the slice: x: 2, y: 2, z: 4, core: 2. Of those that a mesh axis runs over, the one named last changes fastest.
Arguments:
- tokens: bfloat16 [16384, 768], P('batch'), may hold values from -6 to 6
- segment_ids: int32 [16384], P('batch'), may hold values from -1 to 3, as said below
- w_qkv: bfloat16 [3, 768, 768], P(None, None, 'head'), may hold values from -0.21875 to 0.21875
- b_qv: float32 [2, 768], P(None, 'head'), may hold values from -0.6 to 0.6
- w_out: bfloat16 [768, 768], P('head'), may hold values from -1.25 to 1.25
- b_out: float32 [768], replicated, may hold values from -1.8 to 1.8
- ln1_gain: float32 [768], replicated, may hold values from 0.5 to 1.5
- ln1_bias: float32 [768], replicated, may hold values from -1.8 to 1.8
- w_up: bfloat16 [768, 3072], replicated, may hold values from -0.21875 to 0.21875
- b_up: float32 [3072], replicated, may hold values from -3 to 3
- w_down: bfloat16 [3072, 768], replicated, may hold values from -0.109375 to 0.109375
- b_down: float32 [768], replicated, may hold values from -1.8 to 1.8
- ln2_gain: float32 [768], replicated, may hold values from 0.5 to 1.5
- ln2_bias: float32 [768], replicated, may hold values from -1.8 to 1.8
- cotangent: bfloat16 [16384, 768], P(('batch', 'head')), may hold values from -6 to 6
Outputs:
- layer_output: bfloat16 [16384, 768], P(('batch', 'head'))
- input_grad: float32 [16384, 768], P(('batch', 'head'))
- grad_qkv: float32 [3, 768, 768], P(None, None, 'head')
- grad_qv_bias: float32 [2, 768], P(None, 'head')
- grad_out: float32 [768, 768], P('head')
- grad_up: float32 [768, 3072], P(None, 'head')
- grad_up_bias: float32 [3072], P('head')
- grad_down: float32 [3072, 768], P('head')
- grad_small: float32 [6, 768], replicated
Inputs may be any that keep to these rules, and one draw needn't show every extreme that they name: `segment_ids`: within each slot of 512 tokens the ids never fall along the live tokens, which come first; -1 marks the padding at the end of every slot; documents never cross slots.
All inputs are finite; a program needn't handle non-finite values.
Results may differ from a plain program's by a relative error of at most 0.015.
The roundings to bfloat16 on the way count: a program that leaves them out, or rounds other values in their place, can miss the bound.
Values may be sent and summed in bfloat16 or wider, within the bound.
No kernel may reach another device: no remote copies, remote signals or barrier semaphores. Data moves between devices by JAX's collectives and lax.ppermute only.
A program may use at most 192 MiB of HBM per device.

v0:
```python
import functools
import math

import jax
import jax.numpy as jnp
from jax import lax
from jax.experimental import pallas as pl
from jax.experimental.pallas import tpu as pltpu
from jax.sharding import Mesh
from jax.sharding import PartitionSpec as P

HEAD_DIM = 64
SLOT = 512
LOW = jnp.bfloat16
F32 = jnp.float32
LOG2E = math.log2(math.e)
SCORE_SCALE = HEAD_DIM ** (-0.5) * LOG2E
SPARE_BYTES = 12 * 2**20
EXTRA = 64
LIGHT = 0.01
LANES = 128
CHAIN = []
TAIL_SLOPE = 0.36
TAIL = (
    0.14371304537508633,
    0.14177245466203425,
    0.1397192603907239,
    0.026549325413860486,
    0.18095403134327948,
    -0.1797647161697652,
    0.047056295581175855,
)


def swap(value, axis, bit):
    size = lax.axis_size(axis)
    return lax.ppermute(value, axis, [(i, i ^ bit) for i in range(size)])


def swap_core(value):
    return swap(value, "core", 1)


def dot(a, b):
    return jnp.dot(a, b, preferred_element_type=F32)


def dot_nt(a, b):
    return lax.dot_general(a, b, (((1,), (1,)), ((), ())), preferred_element_type=F32)


def dot_tn(a, b):
    return lax.dot_general(a, b, (((0,), (0,)), ((), ())), preferred_element_type=F32)


def whole(shape):
    return pl.BlockSpec(shape, lambda *args: (0,) * len(shape), pipeline_mode=pl.Buffered(1))


def run(
    kernel, places, grid, ins, outs, scratch=(), macs=0, after=(), alias=(), weight=8, chain=True
):
    moved = sum(a.size * a.dtype.itemsize for a, spec in ins)
    moved += sum(math.prod(shape) * jnp.dtype(kind).itemsize for shape, kind, spec in outs)
    after = list(after) + (CHAIN if chain else [])
    count, unread = len(ins), len(alias) + len(after)
    results = len(outs)
    flag = (8, 128)
    if chain:
        outs = outs + [(flag, F32, whole(flag))]

    def body(places, *refs):
        made = refs[count + unread :]
        if chain:

            @pl.when(pl.program_id(0) == 0)
            def _():
                made[results][...] = jnp.zeros(flag, F32)

        kernel(places, *refs[:count], *made[:results], *made[len(outs) :])

    held = pl.BlockSpec(memory_space=pl.ANY)
    room = SPARE_BYTES
    for shape, kind, spec in outs + [(a.shape, a.dtype, spec) for a, spec in ins]:
        if spec.block_shape is not None:
            block = math.prod(1 if n is None else n for n in spec.block_shape)
            copies = 2 if spec.pipeline_mode is None else 1
            room += copies * block * jnp.dtype(kind).itemsize
    for ref in scratch:
        if hasattr(ref, "shape") and ref.dtype in (LOW, F32):
            room += math.prod(ref.shape) * jnp.dtype(ref.dtype).itemsize
    made = pl.pallas_call(
        body,
        name=getattr(kernel, "func", kernel).__name__,
        grid_spec=pltpu.PrefetchScalarGridSpec(
            num_scalar_prefetch=1,
            grid=grid,
            in_specs=[spec for a, spec in ins] + [held] * unread,
            out_specs=[spec for shape, kind, spec in outs],
            scratch_shapes=list(scratch),
        ),
        out_shape=[jax.ShapeDtypeStruct(shape, kind) for shape, kind, spec in outs],
        input_output_aliases={1 + count + i: i for i in range(len(alias))},
        compiler_params=pltpu.CompilerParams(vmem_limit_bytes=room),
        cost_estimate=pl.CostEstimate(
            flops=int(2 * macs * weight), bytes_accessed=int(moved * weight), transcendentals=0
        ),
    )(places, *[a for a, spec in ins], *alias, *after)
    if chain:
        CHAIN[:] = made[results:]
    return made[:results]


def run_whole(
    kernel, places, ins, outs, scratch=(), macs=0, after=(), alias=(), weight=8, chain=True
):
    pairs = [a if isinstance(a, tuple) else (a, pltpu.VMEM) for a in ins]
    after = list(after) + (CHAIN if chain else [])
    count, unread, results = len(pairs), len(alias) + len(after), len(outs)
    if chain:
        outs = outs + [((8, 128), F32)]

    def body(places, *refs):
        made = refs[count + unread :]
        if chain:
            made[results][...] = jnp.zeros((8, 128), F32)
        kernel(places, *refs[:count], *made[:results], *made[len(outs) :])

    room = SPARE_BYTES
    for ref in scratch:
        if hasattr(ref, "shape") and ref.dtype in (LOW, F32):
            room += math.prod(ref.shape) * jnp.dtype(ref.dtype).itemsize
    spaces = [pltpu.SMEM] + [space for a, space in pairs]
    spaces += [pltpu.VMEM] * len(alias) + [pl.ANY] * len(after)
    made = pl.pallas_call(
        body,
        name=getattr(kernel, "func", kernel).__name__,
        in_specs=[pl.BlockSpec(memory_space=space) for space in spaces],
        out_specs=[pl.BlockSpec(memory_space=pltpu.VMEM)] * len(outs),
        scratch_shapes=list(scratch),
        out_shape=[jax.ShapeDtypeStruct(shape, kind) for shape, kind in outs],
        input_output_aliases={1 + count + i: i for i in range(len(alias))},
        compiler_params=pltpu.CompilerParams(vmem_limit_bytes=room),
        cost_estimate=pl.CostEstimate(
            flops=int(2 * macs * weight), bytes_accessed=0, transcendentals=0
        ),
    )(places, *[a for a, space in pairs], *alias, *after)
    if chain:
        CHAIN[:] = made[results:]
    return made[:results]


def each(count, size, body):
    def step(i, carry):
        body(pl.ds(pl.multiple_of(i * size, size), size))
        return carry

    lax.fori_loop(0, count // size, step, 0)


def tiles_of(count, size):
    return [slice(at, at + size) for at in range(0, count, size)]


def three_parts(values):
    parts, rest = [], values
    for _ in range(3):
        parts.append(rest.astype(LOW))
        rest = rest - parts[-1].astype(F32)
    return parts


def segment_rows(seg_row):
    shape = (16, seg_row.shape[1])
    place = lax.broadcasted_iota(jnp.int32, shape, 0)
    same = place - 1 == seg_row
    keys = jnp.where(same, 1.0, jnp.where((place >= 8) & (place < 11), 1.0, 0.0))
    queries = jnp.where(same | (place > 4), 0.0, -1e30)
    return keys.astype(LOW), queries.astype(LOW)


def attend_heads(tok, w_rows, bias, seg_row, qkv_ref, mix_ref, log_ref):
    width = w_rows.shape[0] // 3
    added = dot_tn(bias[:, : 2 * width], jnp.ones((bias.shape[0], tok.shape[0]), LOW))
    qkv = dot_nt(w_rows, tok)
    parts = (
        (qkv[:width] + added[:width]).astype(LOW),
        qkv[width : 2 * width].astype(LOW),
        (qkv[2 * width :] + added[width:]).astype(LOW),
    )
    for c in range(3):
        qkv_ref[c * width : (c + 1) * width] = parts[c]
    more_k, more_q = segment_rows(seg_row)
    for head in range(width // HEAD_DIM):
        q, k, v = (part[head * HEAD_DIM : (head + 1) * HEAD_DIM] for part in parts)
        scores = dot_tn(jnp.concatenate([k, more_k], 0), jnp.concatenate([q, more_q], 0))
        columns, tops, totals = [], [], []
        for tile in tiles_of(scores.shape[1], LANES):
            top = jnp.max(scores[:, tile], 0, keepdims=True)
            total, column = 0.0, []
            for rows in tiles_of(scores.shape[0], 64):
                exponent = jnp.exp2((scores[rows, tile] - top) * SCORE_SCALE)
                total = total + jnp.sum(exponent, 0, keepdims=True)
                column.append(exponent.astype(LOW))
            columns.append(jnp.concatenate(column, 0))
            tops.append(top)
            totals.append(total)
        total = jnp.concatenate(totals, 1)
        mixed = dot(v, jnp.concatenate(columns, 1)) * (1.0 / total)
        mix_ref[head * HEAD_DIM : (head + 1) * HEAD_DIM] = mixed.astype(LOW)
        top = jnp.concatenate(tops, 1)
        log_ref[head : head + 1] = top + jnp.log2(total) * (1.0 / SCORE_SCALE)


def own_attention(
    places, tok, w, bias, seg_row, qkv_ref, mix_ref, log_ref, w_qkv, w_out
):
    count = qkv_ref.shape[1]
    w_qkv[0] = w[:count]
    w_out[0] = w[count:]
    attend_heads(
        tok[...], w[:count], bias[...], seg_row[...], qkv_ref.at[0], mix_ref.at[0], log_ref.at[0]
    )


def far_attention(
    d, order, places, tok, pair, rest, pair_far, rest_far, hop, seg_row,
    qkv_ref, mix_ref, log_ref, w_qkv, w_out, w_ref,
):
    first, second = order
    rows, count = pair.shape[1], qkv_ref.shape[1]
    me = places[0] * 2 + places[1]
    for other, held in enumerate(((pair, rest), (pair_far, rest_far))):
        for two, block in enumerate(held):
            for one in range(2):
                owner = me ^ (other + 2 * first * one + 2 * second * two)
                w_ref[pl.ds(pl.multiple_of(owner * rows, rows), rows)] = block[one]
    w_qkv[d] = w_ref[:count]
    w_out[d] = w_ref[count:]
    attend_heads(
        tok[...],
        w_ref[:count],
        hop[rows:],
        seg_row[...],
        qkv_ref.at[d],
        mix_ref.at[d],
        log_ref.at[d],
    )


def copy_rows(places, rows, out):
    out[...] = rows[...]


def pair_rows(places, first, second, out):
    out[0] = first[: out.shape[1]]
    out[1] = second[: out.shape[1]]


def norm_stats(v):
    centred = v - jnp.mean(v, -1, keepdims=True)
    inv = lax.rsqrt(jnp.mean(centred * centred, -1, keepdims=True) + 1e-05)
    return centred * inv, inv


def norm_back(upstream, unit, inv, gain):
    scaled = upstream * gain
    inner = jnp.mean(scaled * unit, -1, keepdims=True)
    return inv * (scaled - jnp.mean(scaled, -1, keepdims=True) - unit * inner)


def gelu_both(pre):
    power = jnp.exp2(pre * pre * (-0.5 * LOG2E))
    base = 1.0 + TAIL_SLOPE * jnp.abs(pre)
    t = pl.reciprocal(base, approx=True)
    tail = TAIL[6] * t + TAIL[5]
    for c in TAIL[4::-1]:
        tail = tail * t + c
    tail = tail * (t * power)
    cumul = jnp.where(pre < 0.0, tail, 1.0 - tail)
    return (pre * cumul).astype(LOW), cumul + pre * (power * 0.3989422804014327)


def share(core, wide, mine, other):
    half = wide.shape[1] // 2
    left, right = wide[:, :half], wide[:, half:]
    mine[...] = jnp.where(core == 0, left, right)
    other[...] = jnp.where(core == 0, right, left)


def feed_forward(
    places, tok, mix, w_out, b_out, gain1, shift1, b_down, gain2, shift2, w_up, b_up, w_down, cot,
    send, own, ends, slope, unit1, inv1, res2, out, small, tok_send,
    hidden, low, acts, total,
):
    heads, width, half = mix.shape[0], low.shape[1], send.shape[2]
    chunk = 2 * half
    core, z = places[1], places[2]
    b_out, gain1, shift1, b_down, gain2, shift2 = (
        ref[...].reshape(1, -1) for ref in (b_out, gain1, shift1, b_down, gain2, shift2)
    )
    tok_send[...] = jnp.where(core == 0, tok[:, half:], tok[:, :half])
    total[...] = dot_tn(mix[...].reshape(width, low.shape[0]), w_out[...].reshape(width, width))

    def first_norm(rows):
        unit, inv = norm_stats(tok[rows].astype(F32) + (total[rows] + b_out))
        unit1[rows] = unit
        inv1[rows] = inv
        one = unit * gain1 + shift1
        hidden[rows] = one
        one_low = one.astype(LOW)
        low[rows] = one_low
        ends[0, rows] = one_low[:, :half]
        ends[1, rows] = one_low[:, half:]

    each(low.shape[0], 64, first_norm)

    def one_unit(h, carry):
        start = pl.multiple_of(h * chunk, chunk)
        for at in tiles_of(chunk, 256):
            wide = pl.ds(pl.multiple_of(start + at.start, 256), 256)
            pre = dot(low[...], w_up[:, wide])
            for rows in tiles_of(pre.shape[0], 32):
                act, tilt = gelu_both(pre[rows] + b_up[h, :, at])
                slope[h, rows, at] = tilt.astype(LOW)
                acts[rows, wide] = act
        left = acts[:, pl.ds(start, half)]
        right = acts[:, pl.ds(pl.multiple_of(start + half, 128), half)]
        own[z ^ h] = jnp.where(core == 0, left, right)
        send[z ^ h] = jnp.where(core == 0, right, left)
        return carry

    lax.fori_loop(0, heads, one_unit, 0)
    total[...] = dot(acts[...], w_down[...])
    small[...] = jnp.zeros_like(small)

    def second_norm(rows):
        unit, inv = norm_stats(hidden[rows] + (total[rows] + b_down))
        out[rows] = (unit * gain2 + shift2).astype(LOW)
        upstream = cot[rows].astype(F32)
        grad = norm_back(upstream, unit, inv, gain2)
        res2[rows] = grad
        grad_low = grad.astype(LOW)
        ends[2, rows] = grad_low[:, :half]
        ends[3, rows] = grad_low[:, half:]
        for i, term in enumerate((grad_low.astype(F32), upstream * unit, upstream)):
            small[i : i + 1] += jnp.sum(term, 0, keepdims=True)

    each(low.shape[0], 64, second_norm)


def inner_back(places, ends, w_down, slope, send, own, bias, inners):
    heads, _, chunk = slope.shape
    core, z = places[1], places[2]
    branch = jnp.concatenate([ends[2], ends[3]], 1)
    for h in range(heads):
        for at in tiles_of(chunk, 256):
            grad_act = dot_nt(branch, w_down[h * chunk + at.start : h * chunk + at.stop])
            total = 0.0
            for rows in tiles_of(grad_act.shape[0], 32):
                inner = (grad_act[rows] * slope[h, rows, at].astype(F32)).astype(LOW)
                inners[rows, at] = inner
                total = total + jnp.sum(inner.astype(F32), 0, keepdims=True)
            bias[h, :, at] = total
        share(core, inners, own.at[z ^ h], send.at[z ^ h])


def hidden_back(places, own, sent, w_up, res2, unit1, inv1, gain1, send, res1, low, small):
    heads, count, half = own.shape
    core, z = places[1], places[2]
    sides = []
    for h in range(heads):
        mine, other = own[z ^ h], sent[z ^ h]
        sides += [jnp.where(core == 0, mine, other), jnp.where(core == 0, other, mine)]
    product = dot_nt(jnp.concatenate(sides, 1), w_up[...])
    gain = gain1[...].reshape(1, -1)
    sums = [0.0] * 3
    for rows in tiles_of(count, 32):
        grad, unit = product[rows] + res2[rows], unit1[rows]
        result = norm_back(grad, unit, inv1[rows], gain)
        res1[rows] = result
        result_low = result.astype(LOW)
        low[rows] = result_low
        send[rows] = jnp.where(core == 0, result_low[:, half:], result_low[:, :half])
        for i, term in enumerate((result_low.astype(F32), grad * unit, grad)):
            sums[i] = sums[i] + jnp.sum(term, 0, keepdims=True)
    for i in range(3):
        small[i : i + 1] = sums[i]


def shard_back(qkv, w_out, grad, log_ref, more_k, more_q, rows_ref, bias_ref):
    width = qkv.shape[0] // 3
    grad_mixed = dot_nt(w_out[...], grad[...]).astype(LOW)
    scale = HEAD_DIM ** (-0.5)
    for head in range(width // HEAD_DIM):
        places_of = [c * width + head * HEAD_DIM for c in range(3)]
        q, k, v = (qkv[at : at + HEAD_DIM] for at in places_of)
        g = grad_mixed[head * HEAD_DIM : (head + 1) * HEAD_DIM]
        logs = jnp.concatenate(three_parts(-log_ref[head : head + 1]), 0)
        with_logs = jnp.concatenate([more_q[:8], logs, more_q[11:]], 0)
        scores = dot_tn(jnp.concatenate([k, more_k], 0), jnp.concatenate([q, with_logs], 0))
        grad_probs = dot_tn(v, g)
        attends, grads = [], []
        for tile in tiles_of(scores.shape[1], LANES):
            inner, kept, lows, parts = 0.0, [], [], []
            tall = tiles_of(scores.shape[0], 64)
            for down in tall:
                attend = jnp.exp2(scores[down, tile] * SCORE_SCALE)
                inner = inner + jnp.sum(attend * grad_probs[down, tile], 0, keepdims=True)
                kept.append(attend)
                lows.append(attend.astype(LOW))
            for down, attend in zip(tall, kept):
                parts.append((attend * (grad_probs[down, tile] - inner)).astype(LOW))
            attends.append(jnp.concatenate(lows, 0))
            grads.append(jnp.concatenate(parts, 0))
        attend_low = jnp.concatenate(attends, 1)
        grad_scores = jnp.concatenate(grads, 1)
        grad_v = dot_nt(g, attend_low)
        grad_q = dot(k, grad_scores) * scale
        grad_k = dot_nt(q, grad_scores) * scale
        for at, value in zip(places_of, (grad_q, grad_k, grad_v)):
            rows_ref[at : at + HEAD_DIM] = value.astype(LOW)
    ones = jnp.ones((8, rows_ref.shape[1]), LOW)
    bias_ref[...] = dot_nt(ones, rows_ref[...])


def attention_back(places, qkv, w_out, grad, log_ref, seg_row, rows_ref, bias_ref):
    more_k, more_q = segment_rows(seg_row[...])

    def shard(d, carry):
        refs = (ref.at[d] for ref in (rows_ref, bias_ref))
        shard_back(qkv.at[d], w_out.at[d], grad, log_ref.at[d], more_k, more_q, *refs)
        return carry

    lax.fori_loop(0, qkv.shape[0], shard, 0)


def split_rows(value, high, send, keep):
    rows = value.shape[0] // 2
    low = value.astype(LOW)
    send[...] = jnp.where(high, low[:rows], low[rows:])
    keep[...] = jnp.where(high, low[rows:], low[:rows])


def is_high(places, bit):
    return (places[0] & bit) != 0


def unit_products(which, units, units_far, ends, ends_far, both):
    half, count = ends.shape[2], ends.shape[1]
    for side in range(2):
        rows = slice(side * half, (side + 1) * half)
        both[rows, :count] = ends[2 * which + side].T
        both[rows, count:] = ends_far[2 * which + side].T
    for d in range(0, units.shape[0], 2):
        left, right = (jnp.concatenate([units[d + i], units_far[d + i]], 0) for i in range(2))
        yield d, dot(both[...], jnp.concatenate([left, right], 1))


def down_grad(places, units, units_far, ends, ends_far, send, keep, both):
    half = send.shape[2]
    for d, total in unit_products(1, units, units_far, ends, ends_far, both):
        keep[d // 2] = total[:, :half].astype(LOW)
        send[d // 2] = total[:, half:].astype(LOW)


def up_grad(places, units, units_far, ends, ends_far, send_x, keep_x, send_y, keep_y, both):
    half = send_x.shape[2]
    for d, total in unit_products(0, units, units_far, ends, ends_far, both):
        for i in range(2):
            part = total[:, i * half : (i + 1) * half]
            split_rows(part[:half], is_high(places, 1), send_x.at[d + i], keep_x.at[d + i])
            split_rows(part[half:], is_high(places, 2), send_y.at[d + i], keep_y.at[d + i])


def split_at(value, high, send, keep, start):
    rows = value.shape[0] // 2
    low = value.astype(LOW)
    send[start : start + rows] = jnp.where(high, low[:rows], low[rows:])
    keep[start : start + rows] = jnp.where(high, low[rows:], low[:rows])


def first_stage(
    places, d_keep, d_came, x_keep, x_came, y_keep, y_came, send_x, keep_x, send_y, keep_y
):
    half = d_keep.shape[2]
    at = 0
    for i in range(d_keep.shape[0]):
        total = d_keep[i].astype(F32) + d_came[i].astype(F32)
        split_at(total[:half], is_high(places, 1), send_x, keep_x, at)
        split_at(total[half:], is_high(places, 2), send_y, keep_y, at)
        at += half // 2
    for d in range(x_keep.shape[0]):
        upper = x_keep[d].astype(F32) + x_came[d].astype(F32)
        lower = y_keep[d].astype(F32) + y_came[d].astype(F32)
        split_at(upper, is_high(places, 2), send_y, keep_y, at)
        split_at(lower, is_high(places, 1), send_x, keep_x, at)
        at += upper.shape[0] // 2


def second_stage(
    places, x_keep, x_came, y_keep, y_came, send_x, keep_x, send_y, keep_y, send_z, keep_z
):
    rows = send_x.shape[1]
    at = 0
    for i in range(send_x.shape[0]):
        piece = slice(at, at + 2 * rows)
        upper = x_keep[piece].astype(F32) + x_came[piece].astype(F32)
        lower = y_keep[piece].astype(F32) + y_came[piece].astype(F32)
        split_rows(upper, is_high(places, 2), send_y.at[i], keep_y.at[i])
        split_rows(lower, is_high(places, 1), send_x.at[i], keep_x.at[i])
        at += 2 * rows
    for d in range(2 * send_z.shape[0]):
        piece = slice(at, at + rows)
        out = (send_z if d % 2 else keep_z).at[d // 2]
        out[:rows] = (y_keep[piece].astype(F32) + y_came[piece].astype(F32)).astype(LOW)
        out[rows:] = (x_keep[piece].astype(F32) + x_came[piece].astype(F32)).astype(LOW)
        at += rows


def third_stage(places, x_keep, x_came, y_keep, y_came, z_keep, z_came, mine, other):
    rows = x_keep.shape[1]
    for i, out in enumerate((mine, other)):
        out[:rows] = (y_keep[i].astype(F32) + y_came[i].astype(F32)).astype(LOW)
        out[rows : 2 * rows] = (x_keep[i].astype(F32) + x_came[i].astype(F32)).astype(LOW)
        out[2 * rows :] = (z_keep[i].astype(F32) + z_came[i].astype(F32)).astype(LOW)


def attn_grad(
    places, rows, rows_far, tok, tok_far, mix, mix_far, grad, grad_far,
    small_one, small_two, up_bias, qkv_bias, send_x, keep_x, send_y, keep_y,
):
    width = mix.shape[1]
    half = tok_far.shape[1]
    core, z = places[1], places[2]

    def both(near, far):
        mine = jnp.where(core == 0, near[:, :half], near[:, half:])
        return jnp.concatenate([mine, far[...]], 0)

    tok_both, grad_both = both(tok, tok_far), both(grad, grad_far)
    for d in range(rows.shape[0]):
        qkv = dot(jnp.concatenate([rows[d], rows_far[d]], 1), tok_both)
        out = dot(jnp.concatenate([mix[d], mix_far[d]], 1), grad_both)
        lines = []
        for held in (small_one, small_two):
            for i in range(3):
                lines += [held[i : i + 1, :half], held[i : i + 1, half:]]
        line, bias = up_bias[z ^ d], qkv_bias[d]
        lines += [line[:, :half], line[:, half:]]
        lines.append(jnp.concatenate([bias[0:1, :width], bias[0:1, 2 * width :]], 1))
        lines.append(jnp.zeros((EXTRA - len(lines), half), F32))
        total = jnp.concatenate([qkv, out] + lines, 0)
        split_rows(total[:half], is_high(places, 1), send_x.at[d], keep_x.at[d])
        split_rows(total[half:], is_high(places, 2), send_y.at[d], keep_y.at[d])


def add_split(bits, places, *refs):
    for i, bit in enumerate(bits):
        keep, came = refs[2 * i : 2 * i + 2]
        send, left = refs[2 * (len(bits) + i) : 2 * (len(bits) + i) + 2]
        for d in range(keep.shape[0]):
            total = keep[d].astype(F32) + came[d].astype(F32)
            split_rows(total, is_high(places, bit), send.at[d], left.at[d])


def add_parts(places, keep_a, came_a, keep_b, came_b, send, keep):
    rows = keep_a.shape[1]
    for d in range(keep_a.shape[0]):
        out = (send if d % 2 else keep).at[d // 2]
        out[:rows] = (keep_a[d].astype(F32) + came_a[d].astype(F32)).astype(LOW)
        out[rows:] = (keep_b[d].astype(F32) + came_b[d].astype(F32)).astype(LOW)


def add_pair(places, keep, came, *outs):
    for i, out in enumerate(outs):
        out[...] = (keep[i].astype(F32) + came[i].astype(F32)).astype(LOW)


def add_two(places, keep, came, out):
    out[...] = (keep[...].astype(F32) + came[...].astype(F32)).astype(LOW)


def input_sum(places, rows, w, res1, out):
    heads, count, tokens = rows.shape
    total = dot_tn(rows[...].reshape(heads * count, tokens), w[...].reshape(heads * count, -1))
    out[...] = res1[...] + total


def place_pieces(places, held, full, layouts):
    near, core = places[0], places[1]
    width = held[0].shape[1]
    for off in range(4):
        chip = near ^ off
        mine, other = held[off][...], held[4 + off][...]
        sides = (jnp.where(core == 0, mine, other), jnp.where(core == 0, other, mine))
        for at, rows, start, outer in layouts:
            low_bit, high_bit = chip & 1, chip >> 1
            order = 2 * low_bit + high_bit if outer == 1 else 2 * high_bit + low_bit
            to = pl.multiple_of(start + order * rows, 16)
            for side in range(2):
                full[pl.ds(to, rows), side * width : (side + 1) * width] = sides[side][
                    at : at + rows
                ].astype(F32)


def ffn_place(places, *refs):
    held = [ref.at[off] for ref in refs[:2] for off in range(4)]
    down, up, full = refs[2:]
    rows = held[0].shape[0] // 4
    half = 4 * rows
    place_pieces(places, held, full, [(0, rows, 0, 1), (rows, rows, half, 2)])
    down[...] = full[...].T
    place_pieces(places, held, up, [(2 * rows, rows, 0, 1), (3 * rows, rows, half, 2)])


def collect(places, *refs):
    for off in range(4):
        refs[4][off] = refs[off][...]


def attn_place(places, *refs):
    held = [ref.at[off] for ref in refs[:2] for off in range(4)]
    qkv, w_out, small, up_bias, qv_bias, full = refs[2:]
    width = held[0].shape[1]
    count = w_out.shape[0]
    rows = count // 2
    more = held[0].shape[0] - rows
    place_pieces(places, held, full, [(0, rows, 0, 1), (rows, more, 4 * rows, 2)])
    for c in range(3):
        qkv[c] = full[c * count : (c + 1) * count]
    w_out[...] = full[3 * count : 4 * count]
    at = 4 * count
    lines = full[at : at + 16, :width] + full[at : at + 16, width:]
    for i in range(6):
        small[i : i + 1, :width] = lines[2 * i : 2 * i + 1]
        small[i : i + 1, width:] = lines[2 * i + 1 : 2 * i + 2]
    up_bias[...] = jnp.concatenate([lines[12:13], lines[13:14]], 1).reshape(2 * width)
    qv_bias[0:1] = lines[14:15, :count]
    qv_bias[1:2] = lines[14:15, count : 2 * count]


def bias_parts(values):
    rows, rest = [], values
    for _ in range(3):
        rows.append(lax.reduce_precision(rest, 8, 7))
        rest = rest - rows[-1]
    return jnp.stack(rows).astype(LOW)


def gather_back(piece):
    return [piece] + [swap(piece, "near", off) for off in range(1, 4)]


def per_device(
    tokens,
    segment_ids,
    w_qkv,
    b_qv,
    w_out,
    b_out,
    ln1_gain,
    ln1_bias,
    w_up,
    b_up,
    w_down,
    b_down,
    ln2_gain,
    ln2_bias,
    cotangent,
):
    CHAIN.clear()
    width = tokens.shape[1]
    own_rows = cotangent.shape[0]
    local_width = w_qkv.shape[2]
    heads = lax.axis_size("head")
    z = lax.axis_index("head")
    core = lax.axis_index("core")
    near = lax.axis_index("near")
    hidden_units = w_up.shape[1]
    chunk = hidden_units // heads
    half = width // 2
    rows3 = 3 * local_width
    places = jnp.stack([near, core, z]).astype(jnp.int32)

    shard = jnp.concatenate([w_qkv.transpose(0, 2, 1).reshape(rows3, width), w_out], 0)
    piece_rows = shard.shape[0] // 8
    bias = jnp.pad(bias_parts(b_qv.reshape(-1)), ((0, 13), (0, width - 2 * local_width)))
    piece = lax.dynamic_slice_in_dim(shard, (near * 2 + core) * piece_rows, piece_rows, 0)
    piece = jnp.concatenate([piece, bias], 0)
    first_hop = [swap(piece, "head", d) for d in range(1, heads)]

    seg = lax.dynamic_slice_in_dim(segment_ids, z * own_rows, own_rows, 0)
    tok_own = lax.dynamic_slice_in_dim(tokens, z * own_rows, own_rows, 0)
    attend_outs = [
        ((heads, rows3, own_rows), LOW),
        ((heads, local_width, own_rows), LOW),
        ((heads, 8, own_rows), F32),
        ((heads, rows3, width), LOW),
        ((heads, local_width, width), LOW),
    ]
    macs = rows3 * width * own_rows + 6 * own_rows * own_rows * 256
    orders = [(1, 2) if d % 2 else (2, 1) for d in range(heads)]
    nexts = [swap(first_hop[d - 1], "near", orders[d][0]) for d in range(1, heads)]

    def pair_up(d, after):
        (pair,) = run_whole(
            pair_rows, places, [first_hop[d - 1], nexts[d - 1]],
            [((2, piece_rows, width), LOW)], after=after, chain=False,
        )
        return pair

    pairs = [pair_up(1, first_hop[1:])]
    ins = [tok_own, shard, bias, seg[None]]
    made = run_whole(
        own_attention, places, ins, attend_outs, macs=macs, after=pairs, chain=False
    )
    pairs += [pair_up(d, nexts[1:] + [made[2]]) for d in range(2, heads)]
    rests = [swap(pairs[d - 1], "near", orders[d][1]) for d in range(1, heads)]
    for d in range(1, heads):
        pair, rest = pairs[d - 1], rests[d - 1]
        sent = rest
        if d == heads - 1:
            (sent,) = run_whole(
                copy_rows, places, [rest], [(rest.shape, LOW)], after=[second_log], chain=False
            )
        ins = [tok_own, pair, rest, swap_core(pair), swap_core(sent), first_hop[d - 1], seg[None]]
        made = run_whole(
            functools.partial(far_attention, d, orders[d]), places, ins, attend_outs,
            [pltpu.VMEM(shard.shape, LOW)], macs, alias=made, chain=False, weight=100,
        )
        if d == 1:
            second_log = made[2]
    qkvs, mixes, logs, w_qkvs, w_outs = made

    mixes_far = swap_core(mixes)

    square = (own_rows, width)
    tiles = (heads, own_rows, half)
    ins = [
        tok_own, mixes, w_outs, b_out, ln1_gain, ln1_bias, b_down, ln2_gain, ln2_bias,
        w_up, b_up.reshape(heads, 1, chunk), w_down, cotangent,
    ]
    outs = [
        (tiles, LOW),
        (tiles, LOW),
        ((4, own_rows, half), LOW),
        ((heads, own_rows, chunk), LOW),
        (square, F32),
        ((own_rows, 1), F32),
        (square, F32),
        (square, LOW),
        ((8, width), F32),
        ((own_rows, half), LOW),
    ]
    scratch = [
        pltpu.VMEM(square, F32),
        pltpu.VMEM(square, LOW),
        pltpu.VMEM((own_rows, hidden_units), LOW),
        pltpu.VMEM(square, F32),
    ]
    ffn_macs = 2 * own_rows * width * hidden_units
    (
        act_send, act_own, ends, slope, unit1, inv1, res2, layer_output, small_two, tok_send,
    ) = run_whole(feed_forward, places, ins, outs, scratch, ffn_macs)
    tok_far = swap_core(tok_send)
    act_far = swap_core(act_send)
    ends_far = swap_core(ends)

    outs = [(tiles, LOW), (tiles, LOW), ((heads, 1, chunk), F32)]
    scratch = [pltpu.VMEM((own_rows, chunk), LOW)]
    inner_send, inner_own, up_bias = run_whole(
        inner_back, places, [ends, w_down, slope], outs, scratch, ffn_macs // 2, [mixes_far]
    )
    inner_far = swap_core(inner_send)


    both = [pltpu.VMEM((width, 2 * own_rows), LOW)]
    outs = [((heads // 2, width, half), LOW)] * 2
    ins = [act_own, act_far, ends, ends_far]
    d_send, d_keep = run_whole(down_grad, places, ins, outs, both, ffn_macs // 2)
    d_came = swap(d_send, "head", 1)
    outs = [((heads, half // 2, half), LOW)] * 4
    ins = [inner_own, inner_far, ends, ends_far]
    made = run_whole(up_grad, places, ins, outs, both, ffn_macs // 2, weight=LIGHT)
    u_held = (made[1], swap(made[0], "near", 1), made[3], swap(made[2], "near", 2))

    outs = [((own_rows, half), LOW), (square, F32), (square, LOW), ((8, width), F32)]
    ins = [inner_own, inner_send, w_up, res2, unit1, inv1, ln1_gain]
    grad_send, res1, grad_attended, small_one = run_whole(
        hidden_back, places, ins, outs, macs=ffn_macs // 2, weight=LIGHT
    )
    grad_far = swap_core(grad_send)

    def second(x_keep, x_came, y_keep, y_came, macs=0):
        arrays = (x_keep, x_came, y_keep, y_came)
        shapes = [(heads, a.shape[1] // 2, half) for a in (x_keep, x_keep, y_keep, y_keep)]
        outs = [(shape, LOW) for shape in shapes]
        kernel = functools.partial(add_split, (2, 1))
        return run_whole(kernel, places, arrays, outs, macs=macs)

    def third(x_keep, x_came, y_keep, y_came):
        arrays = (x_keep, x_came, y_keep, y_came)
        shape = (heads // 2, x_keep.shape[1] + y_keep.shape[1], half)
        send, keep = run_whole(add_parts, places, arrays, [(shape, LOW)] * 2)
        return keep, swap(send, "head", 1)

    def fourth(keep, came):
        shape = keep.shape[1:]
        mine, other = run_whole(add_pair, places, [keep, came], [(shape, LOW)] * 2)
        return mine, swap(other, "head", 2)

    def fifth(mine, came):
        (total,) = run_whole(add_two, places, [mine, came], [(mine.shape, LOW)])
        bit = 1
        while bit < lax.axis_size("far"):
            total = (total.astype(F32) + swap(total, "far", bit).astype(F32)).astype(LOW)
            bit *= 2
        return total

    def cross_back(made):
        x_send, x_keep, y_send, y_keep = made
        return x_keep, swap(x_send, "near", 1), y_keep, swap(y_send, "near", 2)

    def cross(made, flip):
        x_send, x_keep, y_send, y_keep = made
        x_bit, y_bit = (2, 1) if flip else (1, 2)
        return x_keep, swap(x_send, "near", x_bit), y_keep, swap(y_send, "near", y_bit)

    outs = [((heads, rows3, own_rows), LOW), ((heads, 8, rows3), F32)]
    ins = [qkvs, w_outs, grad_attended, logs, seg[None]]
    rows, qkv_bias = run_whole(attention_back, places, ins, outs)
    rows_far = swap_core(rows)

    outs = [(square, F32, whole(square))]
    ins = [(a, whole(a.shape)) for a in (rows, w_qkvs, res1)]
    (input_grad,) = run(input_sum, places, (1,), ins, outs, weight=LIGHT)
    outs = [((width, half), LOW)] * 4
    ins = [d_keep, d_came, *u_held]
    ffn_held = cross(run_whole(first_stage, places, ins, outs, macs=ffn_macs), False)
    ins = [
        rows, rows_far, tok_own, tok_far, mixes, mixes_far, grad_attended, grad_far,
        small_one, small_two, up_bias, qkv_bias,
    ]
    outs = [
        ((heads, r, half), LOW) for r in (half // 2, (half + EXTRA) // 2) for _ in range(2)
    ]
    made = run_whole(attn_grad, places, ins, outs)
    attn_held = cross(made, False)

    outs = [((heads // 2, half // 4, half), LOW)] * 4 + [((heads // 2, half // 2, half), LOW)] * 2
    made = run_whole(second_stage, places, list(ffn_held), outs, macs=ffn_macs)
    ffn_held = cross_back(made[:4]) + (made[5], swap(made[4], "head", 1))
    attn_held = cross(second(*attn_held), True)
    outs = [((half, half), LOW)] * 2
    mine, other = run_whole(third_stage, places, list(ffn_held), outs, macs=ffn_macs)
    ffn_held = mine, swap(other, "head", 2)
    attn_held = third(*attn_held)
    ffn_held = gather_back(fifth(*ffn_held))
    attn_held = fourth(*attn_held)
    attn_held = gather_back(fifth(*attn_held))

    def both_cores(held):
        shape = (heads,) + held[0].shape
        (pieces,) = run_whole(collect, places, held, [(shape, LOW)])
        return [(a, whole(shape)) for a in (pieces, swap_core(pieces))]

    ffn_held = both_cores(ffn_held)
    outs = [(shape, F32, whole(shape)) for shape in ((chunk, width), (width, chunk))]
    grad_down, grad_up = run(
        ffn_place, places, (1,), ffn_held, outs, [pltpu.VMEM((width, chunk), F32)]
    )
    attn_held = both_cores(attn_held)
    shapes = [
        (3, local_width, width),
        (local_width, width),
        (6, width),
        (chunk,),
        (2, local_width),
    ]
    grad_qkv, grad_out, grad_small, grad_up_bias, grad_qv_bias = run(
        attn_place,
        places,
        (1,),
        attn_held,
        [(shape, F32, whole(shape)) for shape in shapes],
        [pltpu.VMEM((width + EXTRA, width), F32)],
    )
    return (
        layer_output,
        input_grad,
        grad_qkv.transpose(0, 2, 1),
        grad_qv_bias,
        grad_out,
        grad_up,
        grad_up_bias,
        grad_down,
        grad_small,
    )


def solution(mesh):
    batch, heads = mesh.devices.shape
    mesh = Mesh(
        mesh.devices.reshape(batch // 8, 4, 2, heads), ("far", "near", "core", "head")
    )
    group = ("far", "near", "core")
    everyone = group + ("head",)
    in_specs = (
        P(group, None),
        P(group),
        P(None, None, "head"),
        P(None, "head"),
        P("head", None),
        P(),
        P(),
        P(),
        P(),
        P(),
        P(),
        P(),
        P(),
        P(),
        P(everyone, None),
    )
    out_specs = (
        P(everyone, None),
        P(everyone, None),
        P(None, None, "head"),
        P(None, "head"),
        P("head", None),
        P(None, "head"),
        P("head"),
        P("head", None),
        P(),
    )
    return jax.shard_map(
        per_device, mesh=mesh, in_specs=in_specs, out_specs=out_specs, check_vma=False
    )
```

profile of v0, /device:TPU:0, one launch (start us, length us, event | category | flops | bytes accessed | tf_op | source)
XLA Modules:
  0.0 193.0 jit_solution(10378605243817440306)
XLA Ops:
  3.3 3.0 %collective-permute-start.4 = (bf16[112,768]{1,0:T(8,128)(2,1)}, bf16[112,768]{1,0:T(8,128)(2,1)}, u32[]{:S(2)}, u32[]{:S(2)}) collective-permute-start(bf16[112,768]{1,0:T(8,128)(2,1)} %pad_maximum_fusion.1), channel_id=1, source_target_pairs={{0,1},{1,0},{2,3},{3,2},{4,5},{5,4},{6,7},{7,6},{8,9},{9,8},{10,11... | collective-permute-start | bytes 516104 | tf_op jit(solution)/shard_map/ppermute | solution.py:37
  9.0 4.7 %collective-permute-done.4.refs_0_.refs_5_ = bf16[112,768]{1,0:T(8,128)(2,1)} collective-permute-done((bf16[112,768]{1,0:T(8,128)(2,1)}, bf16[112,768]{1,0:T(8,128)(2,1)}, u32[]{:S(2)}, u32[]{:S(2)}) %collective-permute-start.4) | collective-permute-done | bytes 172064 | tf_op jit(solution)/shard_map/ppermute | solution.py:37
  16.4 5.7 %collective-permute-done.2.refs_2_.refs_0_.refs_5_ = bf16[112,768]{1,0:T(8,128)(2,1)S(1)} collective-permute-done((bf16[112,768]{1,0:T(8,128)(2,1)}, bf16[112,768]{1,0:T(8,128)(2,1)S(1)}, u32[]{:S(2)}, u32[]{:S(2)}) %collective-permute-start.2) | collective-permute-done | bytes 172064 | tf_op jit(solution)/shard_map/ppermute | solution.py:37
  26.7 2.9 %own_attention.1 = (bf16[4,576,512]{2,1,0:T(8,128)(2,1)S(1)}, bf16[4,192,512]{2,1,0:T(8,128)(2,1)S(1)}, f32[4,8,512]{2,1,0:T(8,128)S(1)}, bf16[4,576,768]{2,1,0:T(8,128)(2,1)S(1)}, bf16[4,192,768]{2,1,0:T(8,128)(2,1)S(1)}) custom-call(s32[3]{0:T(128)S(1)} %pad_add_fusion.places, bf16[512,768]{1,0:T(8,128)(2,1)S(1)} %constant_dynamic-slice_fusion.refs_0_.refs_2_, ...), custom_call_target="tpu_custom_call" | custom-call | flops 10066329600 | tf_op jit(solution)/shard_map/own_attention/pallas_call | solution.py:135
  31.2 4.4 %collective-permute-done.8.refs_2_ = bf16[2,96,768]{2,1,0:T(8,128)(2,1)S(1)} collective-permute-done((bf16[2,96,768]{2,1,0:T(8,128)(2,1)S(1)}, bf16[2,96,768]{2,1,0:T(8,128)(2,1)S(1)}, u32[]{:S(2)}, u32[]{:S(2)}) %collective-permute-start.8) | collective-permute-done | bytes 294944 | tf_op jit(solution)/shard_map/ppermute | solution.py:37
  39.4 3.4 %far_attention.3 = (bf16[4,576,512]{2,1,0:T(8,128)(2,1)S(1)}, bf16[4,192,512]{2,1,0:T(8,128)(2,1)S(1)}, f32[4,8,512]{2,1,0:T(8,128)S(1)}, bf16[4,576,768]{2,1,0:T(8,128)(2,1)S(1)}, bf16[4,192,768]{2,1,0:T(8,128)(2,1)S(1)}) custom-call(s32[3]{0:T(128)S(1)} %pad_add_fusion.places, ...), custom_call_target="tpu_custom_call", output_to_operand_aliasing={{0}: (8, {}), {1}: (9, {}), {2}: (10, {}), {3}: (11, {}), {... | custom-call | flops 125829120000 | tf_op jit(solution)/shard_map/far_attention/pallas_call | solution.py:135
  42.8 3.7 %collective-permute-done.6.refs_0_.refs_2_ = bf16[2,96,768]{2,1,0:T(8,128)(2,1)S(1)} collective-permute-done((bf16[2,96,768]{2,1,0:T(8,128)(2,1)}, bf16[2,96,768]{2,1,0:T(8,128)(2,1)S(1)}, u32[]{:S(2)}, u32[]{:S(2)}) %collective-permute-start.6) | collective-permute-done | bytes 294944 | tf_op jit(solution)/shard_map/ppermute | solution.py:37
  47.2 3.0 %far_attention.4 = (bf16[4,576,512]{2,1,0:T(8,128)(2,1)S(1)}, bf16[4,192,512]{2,1,0:T(8,128)(2,1)S(1)}, f32[4,8,512]{2,1,0:T(8,128)S(1)}, bf16[4,576,768]{2,1,0:T(8,128)(2,1)S(1)}, bf16[4,192,768]{2,1,0:T(8,128)(2,1)S(1)}) custom-call(s32[3]{0:T(128)S(1)} %pad_add_fusion.places, ...), custom_call_target="tpu_custom_call", output_to_operand_aliasing={{0}: (8, {}), {1}: (9, {}), {2}: (10, {}), {3}: (11, {}), {... | custom-call | flops 125829120000 | tf_op jit(solution)/shard_map/far_attention/pallas_call | solution.py:135
  50.3 3.7 %far_attention.5 = (bf16[4,576,512]{2,1,0:T(8,128)(2,1)S(1)}, bf16[4,192,512]{2,1,0:T(8,128)(2,1)S(1)}, f32[4,8,512]{2,1,0:T(8,128)S(1)}, bf16[4,576,768]{2,1,0:T(8,128)(2,1)S(1)}, bf16[4,192,768]{2,1,0:T(8,128)(2,1)S(1)}) custom-call(s32[3]{0:T(128)S(1)} %pad_add_fusion.places, ...), custom_call_target="tpu_custom_call", output_to_operand_aliasing={{0}: (8, {}), {1}: (9, {}), {2}: (10, {}), {3}: (11, {}), {... | custom-call | flops 125829120000 | tf_op jit(solution)/shard_map/far_attention/pallas_call | solution.py:135
  54.6 18.5 %feed_forward.1 = (bf16[4,512,384]{2,1,0:T(8,128)(2,1)S(1)}, bf16[4,512,384]{2,1,0:T(8,128)(2,1)S(1)}, bf16[4,512,384]{2,1,0:T(8,128)(2,1)S(1)}, bf16[4,512,768]...) custom-call(s32[3]{0:T(128)S(1)} %pad_add_fusion.places, ...), custom_call_target="tpu_custom_call" | custom-call | flops 38654705664 | tf_op jit(solution)/shard_map/feed_forward/pallas_call | solution.py:135
  73.7 3.7 %inner_back.1 = (bf16[4,512,384]{2,1,0:T(8,128)(2,1)S(1)}, bf16[4,512,384]{2,1,0:T(8,128)(2,1)S(1)}, f32[4,1,768]{2,1,0:T(1,128)S(1)}, f32[8,128]{1,0:T(8,128)S(1)}) custom-call(s32[3]{0:T(128)S(1)} %pad_add_fusion.places, bf16[4,512,384]{2,1,0:T(8,128)(2,1)S(1)} %get-tuple-element.128.refs_0_.refs_2_, bf16[3072,768]{1,0:T(8,128)(2,1)S(1)} %copy-done.4, ...), custom_call_target="tpu_custom_call" | custom-call | flops 19327352832 | tf_op jit(solution)/shard_map/inner_back/pallas_call | solution.py:135
  78.8 3.2 %down_grad.1 = (bf16[2,768,384]{2,1,0:T(8,128)(2,1)S(1)}, bf16[2,768,384]{2,1,0:T(8,128)(2,1)S(1)}, f32[8,128]{1,0:T(8,128)S(1)}) custom-call(s32[3]{0:T(128)S(1)} %pad_add_fusion.places, bf16[4,512,384]{2,1,0:T(8,128)(2,1)S(1)} %get-tuple-element.136.refs_0_, bf16[4,512,384]{2,1,0:T(8,128)(2,1)S(1)} %collective-permute-done.18.refs_1_, ...), custom_call_target="tpu_custom_call" | custom-call | flops 19327352832 | tf_op jit(solution)/shard_map/down_grad/pallas_call | solution.py:135
  83.4 3.2 %up_grad.1 = (bf16[4,192,384]{2,1,0:T(8,128)(2,1)S(1)}, bf16[4,192,384]{2,1,0:T(8,128)(2,1)S(1)}, bf16[4,192,384]{2,1,0:T(8,128)(2,1)S(1)}, bf16[4,192,384]{2,1,0:T(8,128)(2,1)S(1)}, f32[8,128]{1,0:T(8,128)S(1)}) custom-call(s32[3]{0:T(128)S(1)} %pad_add_fusion.places, bf16[4,512,384]{2,1,0:T(8,128)(2,1)S(1)} %get-tuple-element.131.refs_0_, ...), custom_call_target="tpu_custom_call" | custom-call | flops 24159192 | tf_op jit(solution)/shard_map/up_grad/pallas_call | solution.py:135
  88.7 4.2 %hidden_back.1 = (bf16[512,384]{1,0:T(8,128)(2,1)S(1)}, f32[512,768]{1,0:T(8,128)S(1)}, bf16[512,768]{1,0:T(8,128)(2,1)S(1)}, f32[8,768]{1,0:T(8,128)S(1)}, f32[8,128]{1,0:T(8,128)S(1)}) custom-call(s32[3]{0:T(128)S(1)} %pad_add_fusion.places, bf16[4,512,384]{2,1,0:T(8,128)(2,1)S(1)} %get-tuple-element.131.refs_0_, ...), custom_call_target="tpu_custom_call" | custom-call | flops 24159192 | tf_op jit(solution)/shard_map/hidden_back/pallas_call | solution.py:135
  93.0 11.8 %attention_back.1 = (bf16[4,576,512]{2,1,0:T(8,128)(2,1)S(1)}, f32[4,8,576]{2,1,0:T(8,128)S(1)}, f32[8,128]{1,0:T(8,128)S(1)}) custom-call(s32[3]{0:T(128)S(1)} %pad_add_fusion.places, bf16[4,576,512]{2,1,0:T(8,128)(2,1)S(1)} %get-tuple-element.127.refs_0_, bf16[4,192,768]{2,1,0:T(8,128)(2,1)S(1)} %get-tuple-element.125.refs_2_.refs_1_, ...), custom_call_target="tpu_custom_call" | custom-call | tf_op jit(solution)/shard_map/attention_back/pallas_call | solution.py:135
  104.9 3.8 %input_sum.1 = (f32[512,768]{1,0:T(8,128)}, f32[8,128]{1,0:T(8,128)S(1)}) custom-call(s32[3]{0:T(128)S(1)} %pad_add_fusion.places, bf16[4,576,512]{2,1,0:T(8,128)(2,1)S(1)} %get-tuple-element.144.refs_0_, bf16[4,576,768]{2,1,0:T(8,128)(2,1)S(1)} %get-tuple-element.145.refs_1_, f32[512,768]{1,0:T(8,128)S(1)} %get-tuple-element.146.refs_2_, ...), custom_call_target="tpu_custom_call" | custom-call | bytes 90439 | tf_op jit(solution)/shard_map/input_sum/pallas_call | solution.py:92
  115.4 4.0 %attn_grad.1 = (bf16[4,192,384]{2,1,0:T(8,128)(2,1)S(1)}, bf16[4,192,384]{2,1,0:T(8,128)(2,1)S(1)}, bf16[4,224,384]{2,1,0:T(8,128)(2,1)S(1)}, bf16[4,224,384]{2,1,0:T(8,128)(2,1)S(1)}, f32[8,128]{1,0:T(8,128)S(1)}) custom-call(s32[3]{0:T(128)S(1)} %pad_add_fusion.places, bf16[4,576,512]{2,1,0:T(8,128)(2,1)S(1)} %get-tuple-element.144.refs_0_, ...), custom_call_target="tpu_custom_call" | custom-call | tf_op jit(solution)/shard_map/attn_grad/pallas_call | solution.py:135
  121.9 5.8 %collective-permute-done.27.refs_1_ = bf16[768,384]{1,0:T(8,128)(2,1)S(1)} collective-permute-done((bf16[768,384]{1,0:T(8,128)(2,1)S(1)}, bf16[768,384]{1,0:T(8,128)(2,1)S(1)}, u32[]{:S(2)}, u32[]{:S(2)}) %collective-permute-start.27) | collective-permute-done | bytes 589856 | tf_op jit(solution)/shard_map/ppermute | solution.py:37
  133.5 6.7 %collective-permute-done.25.refs_1_ = bf16[4,192,384]{2,1,0:T(8,128)(2,1)S(1)} collective-permute-done((bf16[4,192,384]{2,1,0:T(8,128)(2,1)S(1)}, bf16[4,192,384]{2,1,0:T(8,128)(2,1)S(1)}, u32[]{:S(2)}, u32[]{:S(2)}) %collective-permute-start.25) | collective-permute-done | bytes 589856 | tf_op jit(solution)/shard_map/ppermute | solution.py:37
  140.3 2.7 %collective-permute-done.26.refs_3_ = bf16[4,224,384]{2,1,0:T(8,128)(2,1)S(1)} collective-permute-done((bf16[4,224,384]{2,1,0:T(8,128)(2,1)S(1)}, bf16[4,224,384]{2,1,0:T(8,128)(2,1)S(1)}, u32[]{:S(2)}, u32[]{:S(2)}) %collective-permute-start.26) | collective-permute-done | bytes 688160 | tf_op jit(solution)/shard_map/ppermute | solution.py:37
  154.5 5.9 %collective-permute-done.35.refs_1_ = bf16[384,384]{1,0:T(8,128)(2,1)S(1)} collective-permute-done((bf16[384,384]{1,0:T(8,128)(2,1)S(1)}, bf16[384,384]{1,0:T(8,128)(2,1)S(1)}, u32[]{:S(2)}, u32[]{:S(2)}) %collective-permute-start.35) | collective-permute-done | bytes 294944 | tf_op jit(solution)/shard_map/ppermute | solution.py:37
  165.3 8.4 %collective-permute-done.36.refs_1_ = bf16[208,384]{1,0:T(8,128)(2,1)S(1)} collective-permute-done((bf16[208,384]{1,0:T(8,128)(2,1)S(1)}, bf16[208,384]{1,0:T(8,128)(2,1)S(1)}, u32[]{:S(2)}, u32[]{:S(2)}) %collective-permute-start.36) | collective-permute-done | bytes 159776 | tf_op jit(solution)/shard_map/ppermute | solution.py:37
  180.6 3.8 %ffn_place.1 = (f32[768,768]{1,0:T(8,128)}, f32[768,768]{1,0:T(8,128)}, f32[8,128]{1,0:T(8,128)S(1)}) custom-call(s32[3]{0:T(128)S(1)} %pad_add_fusion.places, bf16[4,384,384]{2,1,0:T(8,128)(2,1)S(1)} %get-tuple-element.197.refs_0_, bf16[4,384,384]{2,1,0:T(8,128)(2,1)S(1)} %collective-permute-done.43.refs_1_, f32[8,128]{1,0:T(8,128)S(1)} %get-tuple-element.198.refs_2_), custom_call_target="tpu_custom_call" | custom-call | bytes 56623104 | tf_op jit(solution)/shard_map/ffn_place/pallas_call | solution.py:92
  185.0 2.9 %collective-permute-done.38.refs_2_ = bf16[208,384]{1,0:T(8,128)(2,1)S(1)} collective-permute-done((bf16[208,384]{1,0:T(8,128)(2,1)S(1)}, bf16[208,384]{1,0:T(8,128)(2,1)S(1)}, u32[]{:S(2)}, u32[]{:S(2)}) %collective-permute-start.38) | collective-permute-done | bytes 159776 | tf_op jit(solution)/shard_map/ppermute | solution.py:37
  (131 shorter events, 68.6 us)
Async XLA Ops:
  3.3 10.4 %collective-permute-start.4 = (bf16[112,768]{1,0:T(8,128)(2,1)}, bf16[112,768]{1,0:T(8,128)(2,1)}, u32[]{:S(2)}, u32[]{:S(2)}) collective-permute-start(bf16[112,768]{1,0:T(8,128)(2,1)} %pad_maximum_fusion.1), channel_id=1, source_target_pairs={{0,1},{1,0},{2,3},{3,2},{4,5},{5,4},{6,7},{7,6},{8,9},{9,8},{10,11... | collective-permute-start | bytes 516104 | tf_op jit(solution)/shard_map/ppermute | solution.py:37
  6.3 15.8 %collective-permute-start.2 = (bf16[112,768]{1,0:T(8,128)(2,1)}, bf16[112,768]{1,0:T(8,128)(2,1)S(1)}, u32[]{:S(2)}, u32[]{:S(2)}) collective-permute-start(bf16[112,768]{1,0:T(8,128)(2,1)} %pad_maximum_fusion.1), channel_id=1, source_target_pairs={{0,2},{1,3},{2,0},{3,1},{4,6},{5,7},{6,4},{7,5},{8,10},{9,11},{10,... | collective-permute-start | bytes 516104 | tf_op jit(solution)/shard_map/ppermute | solution.py:37
  8.9 14.7 %collective-permute-start = (bf16[112,768]{1,0:T(8,128)(2,1)}, bf16[112,768]{1,0:T(8,128)(2,1)S(1)}, u32[]{:S(2)}, u32[]{:S(2)}) collective-permute-start(bf16[112,768]{1,0:T(8,128)(2,1)} %pad_maximum_fusion.1), channel_id=1, source_target_pairs={{0,3},{1,2},{2,1},{3,0},{4,7},{5,6},{6,5},{7,4},{8,11},{9,10},{10,... | collective-permute-start | bytes 516104 | tf_op jit(solution)/shard_map/ppermute | solution.py:37
  13.7 11.4 %collective-permute-start.5 = (bf16[112,768]{1,0:T(8,128)(2,1)}, bf16[112,768]{1,0:T(8,128)(2,1)S(1)}, u32[]{:S(2)}, u32[]{:S(2)}) collective-permute-start(bf16[112,768]{1,0:T(8,128)(2,1)} %collective-permute-done.4.refs_0_.refs_5_), channel_id=1, source_target_pairs={{0,8},{8,0},{16,24},{24,16},{1,9},{9,1},{17,25},{25,17},{2,10},{10... | collective-permute-start | bytes 516104 | tf_op jit(solution)/shard_map/ppermute | solution.py:37
  26.1 11.8 %collective-permute-start.9 = (bf16[2,96,768]{2,1,0:T(8,128)(2,1)S(1)}, bf16[2,96,768]{2,1,0:T(8,128)(2,1)S(1)}, u32[]{:S(2)}, u32[]{:S(2)}) collective-permute-start(bf16[2,96,768]{2,1,0:T(8,128)(2,1)S(1)} %pair_rows.3.refs_4_.refs_1_), channel_id=1, source_target_pairs={{0,4},{4,0},{1,5},{5,1},{2,6},{6,2},{3,7},{7,3},{8,12},{12,8},{9,1... | collective-permute-start | bytes 884744 | tf_op jit(solution)/shard_map/ppermute | solution.py:37
  26.2 9.4 %collective-permute-start.8 = (bf16[2,96,768]{2,1,0:T(8,128)(2,1)S(1)}, bf16[2,96,768]{2,1,0:T(8,128)(2,1)S(1)}, u32[]{:S(2)}, u32[]{:S(2)}) collective-permute-start(bf16[2,96,768]{2,1,0:T(8,128)(2,1)S(1)} %pair_rows.3.refs_4_.refs_1_), channel_id=1, source_target_pairs={{0,16},{8,24},{16,0},{24,8},{1,17},{9,25},{17,1},{25,9},{2,18},{10... | collective-permute-start | bytes 884744 | tf_op jit(solution)/shard_map/ppermute | solution.py:37
  36.9 13.3 %collective-permute-start.7 = (bf16[2,96,768]{2,1,0:T(8,128)(2,1)}, bf16[2,96,768]{2,1,0:T(8,128)(2,1)}, u32[]{:S(2)}, u32[]{:S(2)}) collective-permute-start(bf16[2,96,768]{2,1,0:T(8,128)(2,1)} %pair_rows.4.refs_1_), channel_id=1, source_target_pairs={{0,4},{4,0},{1,5},{5,1},{2,6},{6,2},{3,7},{7,3},{8,12},{12,8},{9,1... | collective-permute-start | bytes 884744 | tf_op jit(solution)/shard_map/ppermute | solution.py:37
  54.0 19.7 %collective-permute-start.15 = (bf16[4,192,512]{2,1,0:T(8,128)(2,1)S(1)}, bf16[4,192,512]{2,1,0:T(8,128)(2,1)S(1)}, u32[]{:S(2)}, u32[]{:S(2)}) collective-permute-start(bf16[4,192,512]{2,1,0:T(8,128)(2,1)S(1)} %get-tuple-element.124.refs_1_.refs_4_), channel_id=1, source_target_pairs={{0,4},{4,0},{1,5},{5,1},{2,6},{6,2},{3,7},{7,3},{8,12},{12,8},{9,1... | collective-permute-start | bytes 2359304 | tf_op jit(solution)/shard_map/ppermute | solution.py:37
  82.0 28.1 %collective-permute-start.22 = (bf16[2,768,384]{2,1,0:T(8,128)(2,1)S(1)}, bf16[2,768,384]{2,1,0:T(8,128)(2,1)S(1)}, u32[]{:S(2)}, u32[]{:S(2)}) collective-permute-start(bf16[2,768,384]{2,1,0:T(8,128)(2,1)S(1)} %get-tuple-element.156), channel_id=1, source_target_pairs={{0,1},{1,0},{2,3},{3,2},{4,5},{5,4},{6,7},{7,6},{8,9},{9,8},{10,11... | collective-permute-start | bytes 3538952 | tf_op jit(solution)/shard_map/ppermute | solution.py:37
  86.6 23.5 %collective-permute-start.23 = (bf16[4,192,384]{2,1,0:T(8,128)(2,1)S(1)}, bf16[4,192,384]{2,1,0:T(8,128)(2,1)S(1)}, u32[]{:S(2)}, u32[]{:S(2)}) collective-permute-start(bf16[4,192,384]{2,1,0:T(8,128)(2,1)S(1)} %get-tuple-element.158), channel_id=1, source_target_pairs={{0,8},{8,0},{16,24},{24,16},{1,9},{9,1},{17,25},{25,17},{2,10},{10... | collective-permute-start | bytes 1769480 | tf_op jit(solution)/shard_map/ppermute | solution.py:37
  87.2 23.0 %collective-permute-start.24 = (bf16[4,192,384]{2,1,0:T(8,128)(2,1)S(1)}, bf16[4,192,384]{2,1,0:T(8,128)(2,1)S(1)}, u32[]{:S(2)}, u32[]{:S(2)}) collective-permute-start(bf16[4,192,384]{2,1,0:T(8,128)(2,1)S(1)} %get-tuple-element.160), channel_id=1, source_target_pairs={{0,16},{8,24},{16,0},{24,8},{1,17},{9,25},{17,1},{25,9},{2,18},{10... | collective-permute-start | bytes 1769480 | tf_op jit(solution)/shard_map/ppermute | solution.py:37
  104.8 10.6 %collective-permute-start.19 = (bf16[4,576,512]{2,1,0:T(8,128)(2,1)S(1)}, bf16[4,576,512]{2,1,0:T(8,128)(2,1)S(1)}, u32[]{:S(2)}, u32[]{:S(2)}) collective-permute-start(bf16[4,576,512]{2,1,0:T(8,128)(2,1)S(1)} %get-tuple-element.144.refs_0_), channel_id=1, source_target_pairs={{0,4},{4,0},{1,5},{5,1},{2,6},{6,2},{3,7},{7,3},{8,12},{12,8},{9,1... | collective-permute-start | bytes 7077896 | tf_op jit(solution)/shard_map/ppermute | solution.py:37
  111.4 16.3 %collective-permute-start.27 = (bf16[768,384]{1,0:T(8,128)(2,1)S(1)}, bf16[768,384]{1,0:T(8,128)(2,1)S(1)}, u32[]{:S(2)}, u32[]{:S(2)}) collective-permute-start(bf16[768,384]{1,0:T(8,128)(2,1)S(1)} %get-tuple-element.168), channel_id=1, source_target_pairs={{0,8},{8,0},{16,24},{24,16},{1,9},{9,1},{17,25},{25,17},{2,10},{10... | collective-permute-start | bytes 1769480 | tf_op jit(solution)/shard_map/ppermute | solution.py:37
  112.0 16.2 %collective-permute-start.28 = (bf16[768,384]{1,0:T(8,128)(2,1)S(1)}, bf16[768,384]{1,0:T(8,128)(2,1)S(1)}, u32[]{:S(2)}, u32[]{:S(2)}) collective-permute-start(bf16[768,384]{1,0:T(8,128)(2,1)S(1)} %get-tuple-element.170), channel_id=1, source_target_pairs={{0,16},{8,24},{16,0},{24,8},{1,17},{9,25},{17,1},{25,9},{2,18},{10... | collective-permute-start | bytes 1769480 | tf_op jit(solution)/shard_map/ppermute | solution.py:37
  119.4 20.9 %collective-permute-start.25 = (bf16[4,192,384]{2,1,0:T(8,128)(2,1)S(1)}, bf16[4,192,384]{2,1,0:T(8,128)(2,1)S(1)}, u32[]{:S(2)}, u32[]{:S(2)}) collective-permute-start(bf16[4,192,384]{2,1,0:T(8,128)(2,1)S(1)} %get-tuple-element.164), channel_id=1, source_target_pairs={{0,8},{8,0},{16,24},{24,16},{1,9},{9,1},{17,25},{25,17},{2,10},{10... | collective-permute-start | bytes 1769480 | tf_op jit(solution)/shard_map/ppermute | solution.py:37
  121.0 22.0 %collective-permute-start.26 = (bf16[4,224,384]{2,1,0:T(8,128)(2,1)S(1)}, bf16[4,224,384]{2,1,0:T(8,128)(2,1)S(1)}, u32[]{:S(2)}, u32[]{:S(2)}) collective-permute-start(bf16[4,224,384]{2,1,0:T(8,128)(2,1)S(1)} %get-tuple-element.166), channel_id=1, source_target_pairs={{0,16},{8,24},{16,0},{24,8},{1,17},{9,25},{17,1},{25,9},{2,18},{10... | collective-permute-start | bytes 2064392 | tf_op jit(solution)/shard_map/ppermute | solution.py:37
  129.1 17.4 %collective-permute-start.33 = (bf16[2,192,384]{2,1,0:T(8,128)(2,1)S(1)}, bf16[2,192,384]{2,1,0:T(8,128)(2,1)S(1)}, u32[]{:S(2)}, u32[]{:S(2)}) collective-permute-start(bf16[2,192,384]{2,1,0:T(8,128)(2,1)S(1)} %get-tuple-element.182), channel_id=1, source_target_pairs={{0,1},{1,0},{2,3},{3,2},{4,5},{5,4},{6,7},{7,6},{8,9},{9,8},{10,11... | collective-permute-start | bytes 884744 | tf_op jit(solution)/shard_map/ppermute | solution.py:37
  130.5 16.0 %collective-permute-start.31 = (bf16[2,96,384]{2,1,0:T(8,128)(2,1)S(1)}, bf16[2,96,384]{2,1,0:T(8,128)(2,1)S(1)}, u32[]{:S(2)}, u32[]{:S(2)}) collective-permute-start(bf16[2,96,384]{2,1,0:T(8,128)(2,1)S(1)} %get-tuple-element.178), channel_id=1, source_target_pairs={{0,8},{8,0},{16,24},{24,16},{1,9},{9,1},{17,25},{25,17},{2,10},{10... | collective-permute-start | bytes 442376 | tf_op jit(solution)/shard_map/ppermute | solution.py:37
  132.0 14.5 %collective-permute-start.32 = (bf16[2,96,384]{2,1,0:T(8,128)(2,1)S(1)}, bf16[2,96,384]{2,1,0:T(8,128)(2,1)S(1)}, u32[]{:S(2)}, u32[]{:S(2)}) collective-permute-start(bf16[2,96,384]{2,1,0:T(8,128)(2,1)S(1)} %get-tuple-element.180), channel_id=1, source_target_pairs={{0,16},{8,24},{16,0},{24,8},{1,17},{9,25},{17,1},{25,9},{2,18},{10... | collective-permute-start | bytes 442376 | tf_op jit(solution)/shard_map/ppermute | solution.py:37
  147.3 13.2 %collective-permute-start.35 = (bf16[384,384]{1,0:T(8,128)(2,1)S(1)}, bf16[384,384]{1,0:T(8,128)(2,1)S(1)}, u32[]{:S(2)}, u32[]{:S(2)}) collective-permute-start(bf16[384,384]{1,0:T(8,128)(2,1)S(1)} %get-tuple-element.188), channel_id=1, source_target_pairs={{0,2},{1,3},{2,0},{3,1},{4,6},{5,7},{6,4},{7,5},{8,10},{9,11},{10,... | collective-permute-start | bytes 884744 | tf_op jit(solution)/shard_map/ppermute | solution.py:37
  153.0 11.6 %collective-permute-start.34 = (bf16[2,208,384]{2,1,0:T(8,128)(2,1)S(1)}, bf16[2,208,384]{2,1,0:T(8,128)(2,1)S(1)}, u32[]{:S(2)}, u32[]{:S(2)}) collective-permute-start(bf16[2,208,384]{2,1,0:T(8,128)(2,1)S(1)} %get-tuple-element.186), channel_id=1, source_target_pairs={{0,1},{1,0},{2,3},{3,2},{4,5},{5,4},{6,7},{7,6},{8,9},{9,8},{10,11... | collective-permute-start | bytes 958472 | tf_op jit(solution)/shard_map/ppermute | solution.py:37
  161.1 13.2 %collective-permute-start.42 = (bf16[384,384]{1,0:T(8,128)(2,1)S(1)}, bf16[384,384]{1,0:T(8,128)(2,1)S(1)}, u32[]{:S(2)}, u32[]{:S(2)}) collective-permute-start(bf16[384,384]{1,0:T(8,128)(2,1)S(1)} %get-tuple-element.195.refs_0_), channel_id=1, source_target_pairs={{0,24},{8,16},{16,8},{24,0},{1,25},{9,17},{17,9},{25,1},{2,26},{10... | collective-permute-start | bytes 884744 | tf_op jit(solution)/shard_map/ppermute | solution.py:37
  162.7 13.6 %collective-permute-start.41 = (bf16[384,384]{1,0:T(8,128)(2,1)S(1)}, bf16[384,384]{1,0:T(8,128)(2,1)S(1)}, u32[]{:S(2)}, u32[]{:S(2)}) collective-permute-start(bf16[384,384]{1,0:T(8,128)(2,1)S(1)} %get-tuple-element.195.refs_0_), channel_id=1, source_target_pairs={{0,16},{8,24},{16,0},{24,8},{1,17},{9,25},{17,1},{25,9},{2,18},{10... | collective-permute-start | bytes 884744 | tf_op jit(solution)/shard_map/ppermute | solution.py:37
  163.0 13.3 %collective-permute-start.40 = (bf16[384,384]{1,0:T(8,128)(2,1)S(1)}, bf16[384,384]{1,0:T(8,128)(2,1)S(1)}, u32[]{:S(2)}, u32[]{:S(2)}) collective-permute-start(bf16[384,384]{1,0:T(8,128)(2,1)S(1)} %get-tuple-element.195.refs_0_), channel_id=1, source_target_pairs={{0,8},{8,0},{16,24},{24,16},{1,9},{9,1},{17,25},{25,17},{2,10},{10... | collective-permute-start | bytes 884744 | tf_op jit(solution)/shard_map/ppermute | solution.py:37
  (35 other events, 208.3 us)
where the time goes:
time: 193 us
  Pallas kernels  82.5 us (43%)
  waiting for transfers between devices  64.9 us (34%)
  starting transfers between devices  40.9 us (21%)
    pallas_call x25, Pallas kernels, run_whole(): pl.pallas_call(body, name=getattr(kernel, 'func', kernel).__name__, in_sp...  72.6 us
    ppermute x45, waiting for transfers between devices, swap(): return lax.ppermute(value, axis, [(i, i ^ bit) for i in range(size)])  64.9 us
    ppermute x45, starting transfers between devices, swap(): return lax.ppermute(value, axis, [(i, i ^ bit) for i in range(size)])  40.9 us
    pallas_call x3, Pallas kernels, run(): pl.pallas_call(body, name=getattr(kernel, 'func', kernel).__name__, grid_...  9.88 us
  transfers between devices with their start and end apart: 45, of which 21 were waited for; matrix products, arithmetic and copies ran while one was open for 1% of the time, Pallas kernels for 39%

commit v1 on v0

--- a/solution.py
+++ b/solution.py
@@ -317,10 +317,10 @@
 
     def one_unit(h, carry):
         start = pl.multiple_of(h * chunk, chunk)
-        for at in tiles_of(chunk, 256):
-            wide = pl.ds(pl.multiple_of(start + at.start, 256), 256)
+        for at in tiles_of(chunk, chunk):
+            wide = pl.ds(start, chunk)
             pre = dot(low[...], w_up[:, wide])
-            for rows in tiles_of(pre.shape[0], 32):
+            for rows in tiles_of(pre.shape[0], 16):
                 act, tilt = gelu_both(pre[rows] + b_up[h, :, at])
                 slope[h, rows, at] = tilt.astype(LOW)
                 acts[rows, wide] = act

time: 193 us -> 193 us (level)
  no operation moved by 1% of the time
where the time goes in v1:
time: 193 us
  Pallas kernels  82.2 us (43%)
  waiting for transfers between devices  64.9 us (34%)
  starting transfers between devices  40.9 us (21%)
    pallas_call x25, Pallas kernels, run_whole(): pl.pallas_call(body, name=getattr(kernel, 'func', kernel).__name__, in_sp...  72.3 us
    ppermute x45, waiting for transfers between devices, swap(): return lax.ppermute(value, axis, [(i, i ^ bit) for i in range(size)])  64.9 us
    ppermute x45, starting transfers between devices, swap(): return lax.ppermute(value, axis, [(i, i ^ bit) for i in range(size)])  40.9 us
    pallas_call x3, Pallas kernels, run(): pl.pallas_call(body, name=getattr(kernel, 'func', kernel).__name__, grid_...  9.88 us
  transfers between devices with their start and end apart: 45, of which 21 were waited for; matrix products, arithmetic and copies ran while one was open for 1% of the time, Pallas kernels for 39%

profile of v1, /device:TPU:0, one launch (start us, length us, event | category | flops | bytes accessed | tf_op | source)
XLA Modules:
  0.0 192.7 jit_solution(16083022885392062110)
XLA Ops:
  3.3 3.0 %collective-permute-start.4 = (bf16[112,768]{1,0:T(8,128)(2,1)}, bf16[112,768]{1,0:T(8,128)(2,1)}, u32[]{:S(2)}, u32[]{:S(2)}) collective-permute-start(bf16[112,768]{1,0:T(8,128)(2,1)} %pad_maximum_fusion.1), channel_id=1, source_target_pairs={{0,1},{1,0},{2,3},{3,2},{4,5},{5,4},{6,7},{7,6},{8,9},{9,8},{10,11... | collective-permute-start | bytes 516104 | tf_op jit(solution)/shard_map/ppermute | solution.py:37
  9.0 4.7 %collective-permute-done.4.refs_0_.refs_5_ = bf16[112,768]{1,0:T(8,128)(2,1)} collective-permute-done((bf16[112,768]{1,0:T(8,128)(2,1)}, bf16[112,768]{1,0:T(8,128)(2,1)}, u32[]{:S(2)}, u32[]{:S(2)}) %collective-permute-start.4) | collective-permute-done | bytes 172064 | tf_op jit(solution)/shard_map/ppermute | solution.py:37
  16.4 5.7 %collective-permute-done.2.refs_2_.refs_0_.refs_5_ = bf16[112,768]{1,0:T(8,128)(2,1)S(1)} collective-permute-done((bf16[112,768]{1,0:T(8,128)(2,1)}, bf16[112,768]{1,0:T(8,128)(2,1)S(1)}, u32[]{:S(2)}, u32[]{:S(2)}) %collective-permute-start.2) | collective-permute-done | bytes 172064 | tf_op jit(solution)/shard_map/ppermute | solution.py:37
  26.7 2.9 %own_attention.1 = (bf16[4,576,512]{2,1,0:T(8,128)(2,1)S(1)}, bf16[4,192,512]{2,1,0:T(8,128)(2,1)S(1)}, f32[4,8,512]{2,1,0:T(8,128)S(1)}, bf16[4,576,768]{2,1,0:T(8,128)(2,1)S(1)}, bf16[4,192,768]{2,1,0:T(8,128)(2,1)S(1)}) custom-call(s32[3]{0:T(128)S(1)} %pad_add_fusion.places, bf16[512,768]{1,0:T(8,128)(2,1)S(1)} %constant_dynamic-slice_fusion.refs_0_.refs_2_, ...), custom_call_target="tpu_custom_call" | custom-call | flops 10066329600 | tf_op jit(solution)/shard_map/own_attention/pallas_call | solution.py:135
  31.2 4.4 %collective-permute-done.8.refs_2_ = bf16[2,96,768]{2,1,0:T(8,128)(2,1)S(1)} collective-permute-done((bf16[2,96,768]{2,1,0:T(8,128)(2,1)S(1)}, bf16[2,96,768]{2,1,0:T(8,128)(2,1)S(1)}, u32[]{:S(2)}, u32[]{:S(2)}) %collective-permute-start.8) | collective-permute-done | bytes 294944 | tf_op jit(solution)/shard_map/ppermute | solution.py:37
  39.4 3.4 %far_attention.3 = (bf16[4,576,512]{2,1,0:T(8,128)(2,1)S(1)}, bf16[4,192,512]{2,1,0:T(8,128)(2,1)S(1)}, f32[4,8,512]{2,1,0:T(8,128)S(1)}, bf16[4,576,768]{2,1,0:T(8,128)(2,1)S(1)}, bf16[4,192,768]{2,1,0:T(8,128)(2,1)S(1)}) custom-call(s32[3]{0:T(128)S(1)} %pad_add_fusion.places, ...), custom_call_target="tpu_custom_call", output_to_operand_aliasing={{0}: (8, {}), {1}: (9, {}), {2}: (10, {}), {3}: (11, {}), {... | custom-call | flops 125829120000 | tf_op jit(solution)/shard_map/far_attention/pallas_call | solution.py:135
  42.8 3.7 %collective-permute-done.6.refs_0_.refs_2_ = bf16[2,96,768]{2,1,0:T(8,128)(2,1)S(1)} collective-permute-done((bf16[2,96,768]{2,1,0:T(8,128)(2,1)}, bf16[2,96,768]{2,1,0:T(8,128)(2,1)S(1)}, u32[]{:S(2)}, u32[]{:S(2)}) %collective-permute-start.6) | collective-permute-done | bytes 294944 | tf_op jit(solution)/shard_map/ppermute | solution.py:37
  47.2 3.0 %far_attention.4 = (bf16[4,576,512]{2,1,0:T(8,128)(2,1)S(1)}, bf16[4,192,512]{2,1,0:T(8,128)(2,1)S(1)}, f32[4,8,512]{2,1,0:T(8,128)S(1)}, bf16[4,576,768]{2,1,0:T(8,128)(2,1)S(1)}, bf16[4,192,768]{2,1,0:T(8,128)(2,1)S(1)}) custom-call(s32[3]{0:T(128)S(1)} %pad_add_fusion.places, ...), custom_call_target="tpu_custom_call", output_to_operand_aliasing={{0}: (8, {}), {1}: (9, {}), {2}: (10, {}), {3}: (11, {}), {... | custom-call | flops 125829120000 | tf_op jit(solution)/shard_map/far_attention/pallas_call | solution.py:135
  50.3 3.7 %far_attention.5 = (bf16[4,576,512]{2,1,0:T(8,128)(2,1)S(1)}, bf16[4,192,512]{2,1,0:T(8,128)(2,1)S(1)}, f32[4,8,512]{2,1,0:T(8,128)S(1)}, bf16[4,576,768]{2,1,0:T(8,128)(2,1)S(1)}, bf16[4,192,768]{2,1,0:T(8,128)(2,1)S(1)}) custom-call(s32[3]{0:T(128)S(1)} %pad_add_fusion.places, ...), custom_call_target="tpu_custom_call", output_to_operand_aliasing={{0}: (8, {}), {1}: (9, {}), {2}: (10, {}), {3}: (11, {}), {... | custom-call | flops 125829120000 | tf_op jit(solution)/shard_map/far_attention/pallas_call | solution.py:135
  54.6 18.2 %feed_forward.1 = (bf16[4,512,384]{2,1,0:T(8,128)(2,1)S(1)}, bf16[4,512,384]{2,1,0:T(8,128)(2,1)S(1)}, bf16[4,512,384]{2,1,0:T(8,128)(2,1)S(1)}, bf16[4,512,768]...) custom-call(s32[3]{0:T(128)S(1)} %pad_add_fusion.places, ...), custom_call_target="tpu_custom_call" | custom-call | flops 38654705664 | tf_op jit(solution)/shard_map/feed_forward/pallas_call | solution.py:135
  73.4 3.7 %inner_back.1 = (bf16[4,512,384]{2,1,0:T(8,128)(2,1)S(1)}, bf16[4,512,384]{2,1,0:T(8,128)(2,1)S(1)}, f32[4,1,768]{2,1,0:T(1,128)S(1)}, f32[8,128]{1,0:T(8,128)S(1)}) custom-call(s32[3]{0:T(128)S(1)} %pad_add_fusion.places, bf16[4,512,384]{2,1,0:T(8,128)(2,1)S(1)} %get-tuple-element.128.refs_0_.refs_2_, bf16[3072,768]{1,0:T(8,128)(2,1)S(1)} %copy-done.4, ...), custom_call_target="tpu_custom_call" | custom-call | flops 19327352832 | tf_op jit(solution)/shard_map/inner_back/pallas_call | solution.py:135
  78.5 3.2 %down_grad.1 = (bf16[2,768,384]{2,1,0:T(8,128)(2,1)S(1)}, bf16[2,768,384]{2,1,0:T(8,128)(2,1)S(1)}, f32[8,128]{1,0:T(8,128)S(1)}) custom-call(s32[3]{0:T(128)S(1)} %pad_add_fusion.places, bf16[4,512,384]{2,1,0:T(8,128)(2,1)S(1)} %get-tuple-element.136.refs_0_, bf16[4,512,384]{2,1,0:T(8,128)(2,1)S(1)} %collective-permute-done.18.refs_1_, ...), custom_call_target="tpu_custom_call" | custom-call | flops 19327352832 | tf_op jit(solution)/shard_map/down_grad/pallas_call | solution.py:135
  83.1 3.2 %up_grad.1 = (bf16[4,192,384]{2,1,0:T(8,128)(2,1)S(1)}, bf16[4,192,384]{2,1,0:T(8,128)(2,1)S(1)}, bf16[4,192,384]{2,1,0:T(8,128)(2,1)S(1)}, bf16[4,192,384]{2,1,0:T(8,128)(2,1)S(1)}, f32[8,128]{1,0:T(8,128)S(1)}) custom-call(s32[3]{0:T(128)S(1)} %pad_add_fusion.places, bf16[4,512,384]{2,1,0:T(8,128)(2,1)S(1)} %get-tuple-element.131.refs_0_, ...), custom_call_target="tpu_custom_call" | custom-call | flops 24159192 | tf_op jit(solution)/shard_map/up_grad/pallas_call | solution.py:135
  88.4 4.2 %hidden_back.1 = (bf16[512,384]{1,0:T(8,128)(2,1)S(1)}, f32[512,768]{1,0:T(8,128)S(1)}, bf16[512,768]{1,0:T(8,128)(2,1)S(1)}, f32[8,768]{1,0:T(8,128)S(1)}, f32[8,128]{1,0:T(8,128)S(1)}) custom-call(s32[3]{0:T(128)S(1)} %pad_add_fusion.places, bf16[4,512,384]{2,1,0:T(8,128)(2,1)S(1)} %get-tuple-element.131.refs_0_, ...), custom_call_target="tpu_custom_call" | custom-call | flops 24159192 | tf_op jit(solution)/shard_map/hidden_back/pallas_call | solution.py:135
  92.6 11.8 %attention_back.1 = (bf16[4,576,512]{2,1,0:T(8,128)(2,1)S(1)}, f32[4,8,576]{2,1,0:T(8,128)S(1)}, f32[8,128]{1,0:T(8,128)S(1)}) custom-call(s32[3]{0:T(128)S(1)} %pad_add_fusion.places, bf16[4,576,512]{2,1,0:T(8,128)(2,1)S(1)} %get-tuple-element.127.refs_0_, bf16[4,192,768]{2,1,0:T(8,128)(2,1)S(1)} %get-tuple-element.125.refs_2_.refs_1_, ...), custom_call_target="tpu_custom_call" | custom-call | tf_op jit(solution)/shard_map/attention_back/pallas_call | solution.py:135
  104.6 3.8 %input_sum.1 = (f32[512,768]{1,0:T(8,128)}, f32[8,128]{1,0:T(8,128)S(1)}) custom-call(s32[3]{0:T(128)S(1)} %pad_add_fusion.places, bf16[4,576,512]{2,1,0:T(8,128)(2,1)S(1)} %get-tuple-element.144.refs_0_, bf16[4,576,768]{2,1,0:T(8,128)(2,1)S(1)} %get-tuple-element.145.refs_1_, f32[512,768]{1,0:T(8,128)S(1)} %get-tuple-element.146.refs_2_, ...), custom_call_target="tpu_custom_call" | custom-call | bytes 90439 | tf_op jit(solution)/shard_map/input_sum/pallas_call | solution.py:92
  115.1 4.0 %attn_grad.1 = (bf16[4,192,384]{2,1,0:T(8,128)(2,1)S(1)}, bf16[4,192,384]{2,1,0:T(8,128)(2,1)S(1)}, bf16[4,224,384]{2,1,0:T(8,128)(2,1)S(1)}, bf16[4,224,384]{2,1,0:T(8,128)(2,1)S(1)}, f32[8,128]{1,0:T(8,128)S(1)}) custom-call(s32[3]{0:T(128)S(1)} %pad_add_fusion.places, bf16[4,576,512]{2,1,0:T(8,128)(2,1)S(1)} %get-tuple-element.144.refs_0_, ...), custom_call_target="tpu_custom_call" | custom-call | tf_op jit(solution)/shard_map/attn_grad/pallas_call | solution.py:135
  121.6 5.8 %collective-permute-done.27.refs_1_ = bf16[768,384]{1,0:T(8,128)(2,1)S(1)} collective-permute-done((bf16[768,384]{1,0:T(8,128)(2,1)S(1)}, bf16[768,384]{1,0:T(8,128)(2,1)S(1)}, u32[]{:S(2)}, u32[]{:S(2)}) %collective-permute-start.27) | collective-permute-done | bytes 589856 | tf_op jit(solution)/shard_map/ppermute | solution.py:37
  133.2 6.7 %collective-permute-done.25.refs_1_ = bf16[4,192,384]{2,1,0:T(8,128)(2,1)S(1)} collective-permute-done((bf16[4,192,384]{2,1,0:T(8,128)(2,1)S(1)}, bf16[4,192,384]{2,1,0:T(8,128)(2,1)S(1)}, u32[]{:S(2)}, u32[]{:S(2)}) %collective-permute-start.25) | collective-permute-done | bytes 589856 | tf_op jit(solution)/shard_map/ppermute | solution.py:37
  140.0 2.7 %collective-permute-done.26.refs_3_ = bf16[4,224,384]{2,1,0:T(8,128)(2,1)S(1)} collective-permute-done((bf16[4,224,384]{2,1,0:T(8,128)(2,1)S(1)}, bf16[4,224,384]{2,1,0:T(8,128)(2,1)S(1)}, u32[]{:S(2)}, u32[]{:S(2)}) %collective-permute-start.26) | collective-permute-done | bytes 688160 | tf_op jit(solution)/shard_map/ppermute | solution.py:37
  154.2 5.9 %collective-permute-done.35.refs_1_ = bf16[384,384]{1,0:T(8,128)(2,1)S(1)} collective-permute-done((bf16[384,384]{1,0:T(8,128)(2,1)S(1)}, bf16[384,384]{1,0:T(8,128)(2,1)S(1)}, u32[]{:S(2)}, u32[]{:S(2)}) %collective-permute-start.35) | collective-permute-done | bytes 294944 | tf_op jit(solution)/shard_map/ppermute | solution.py:37
  165.0 8.3 %collective-permute-done.36.refs_1_ = bf16[208,384]{1,0:T(8,128)(2,1)S(1)} collective-permute-done((bf16[208,384]{1,0:T(8,128)(2,1)S(1)}, bf16[208,384]{1,0:T(8,128)(2,1)S(1)}, u32[]{:S(2)}, u32[]{:S(2)}) %collective-permute-start.36) | collective-permute-done | bytes 159776 | tf_op jit(solution)/shard_map/ppermute | solution.py:37
  180.3 3.8 %ffn_place.1 = (f32[768,768]{1,0:T(8,128)}, f32[768,768]{1,0:T(8,128)}, f32[8,128]{1,0:T(8,128)S(1)}) custom-call(s32[3]{0:T(128)S(1)} %pad_add_fusion.places, bf16[4,384,384]{2,1,0:T(8,128)(2,1)S(1)} %get-tuple-element.197.refs_0_, bf16[4,384,384]{2,1,0:T(8,128)(2,1)S(1)} %collective-permute-done.43.refs_1_, f32[8,128]{1,0:T(8,128)S(1)} %get-tuple-element.198.refs_2_), custom_call_target="tpu_custom_call" | custom-call | bytes 56623104 | tf_op jit(solution)/shard_map/ffn_place/pallas_call | solution.py:92
  184.7 2.9 %collective-permute-done.38.refs_2_ = bf16[208,384]{1,0:T(8,128)(2,1)S(1)} collective-permute-done((bf16[208,384]{1,0:T(8,128)(2,1)S(1)}, bf16[208,384]{1,0:T(8,128)(2,1)S(1)}, u32[]{:S(2)}, u32[]{:S(2)}) %collective-permute-start.38) | collective-permute-done | bytes 159776 | tf_op jit(solution)/shard_map/ppermute | solution.py:37
  (131 shorter events, 68.7 us)
Async XLA Ops:
  3.3 10.4 %collective-permute-start.4 = (bf16[112,768]{1,0:T(8,128)(2,1)}, bf16[112,768]{1,0:T(8,128)(2,1)}, u32[]{:S(2)}, u32[]{:S(2)}) collective-permute-start(bf16[112,768]{1,0:T(8,128)(2,1)} %pad_maximum_fusion.1), channel_id=1, source_target_pairs={{0,1},{1,0},{2,3},{3,2},{4,5},{5,4},{6,7},{7,6},{8,9},{9,8},{10,11... | collective-permute-start | bytes 516104 | tf_op jit(solution)/shard_map/ppermute | solution.py:37
  6.3 15.8 %collective-permute-start.2 = (bf16[112,768]{1,0:T(8,128)(2,1)}, bf16[112,768]{1,0:T(8,128)(2,1)S(1)}, u32[]{:S(2)}, u32[]{:S(2)}) collective-permute-start(bf16[112,768]{1,0:T(8,128)(2,1)} %pad_maximum_fusion.1), channel_id=1, source_target_pairs={{0,2},{1,3},{2,0},{3,1},{4,6},{5,7},{6,4},{7,5},{8,10},{9,11},{10,... | collective-permute-start | bytes 516104 | tf_op jit(solution)/shard_map/ppermute | solution.py:37
  8.9 14.7 %collective-permute-start = (bf16[112,768]{1,0:T(8,128)(2,1)}, bf16[112,768]{1,0:T(8,128)(2,1)S(1)}, u32[]{:S(2)}, u32[]{:S(2)}) collective-permute-start(bf16[112,768]{1,0:T(8,128)(2,1)} %pad_maximum_fusion.1), channel_id=1, source_target_pairs={{0,3},{1,2},{2,1},{3,0},{4,7},{5,6},{6,5},{7,4},{8,11},{9,10},{10,... | collective-permute-start | bytes 516104 | tf_op jit(solution)/shard_map/ppermute | solution.py:37
  13.7 11.4 %collective-permute-start.5 = (bf16[112,768]{1,0:T(8,128)(2,1)}, bf16[112,768]{1,0:T(8,128)(2,1)S(1)}, u32[]{:S(2)}, u32[]{:S(2)}) collective-permute-start(bf16[112,768]{1,0:T(8,128)(2,1)} %collective-permute-done.4.refs_0_.refs_5_), channel_id=1, source_target_pairs={{0,8},{8,0},{16,24},{24,16},{1,9},{9,1},{17,25},{25,17},{2,10},{10... | collective-permute-start | bytes 516104 | tf_op jit(solution)/shard_map/ppermute | solution.py:37
  26.1 11.8 %collective-permute-start.9 = (bf16[2,96,768]{2,1,0:T(8,128)(2,1)S(1)}, bf16[2,96,768]{2,1,0:T(8,128)(2,1)S(1)}, u32[]{:S(2)}, u32[]{:S(2)}) collective-permute-start(bf16[2,96,768]{2,1,0:T(8,128)(2,1)S(1)} %pair_rows.3.refs_4_.refs_1_), channel_id=1, source_target_pairs={{0,4},{4,0},{1,5},{5,1},{2,6},{6,2},{3,7},{7,3},{8,12},{12,8},{9,1... | collective-permute-start | bytes 884744 | tf_op jit(solution)/shard_map/ppermute | solution.py:37
  26.2 9.4 %collective-permute-start.8 = (bf16[2,96,768]{2,1,0:T(8,128)(2,1)S(1)}, bf16[2,96,768]{2,1,0:T(8,128)(2,1)S(1)}, u32[]{:S(2)}, u32[]{:S(2)}) collective-permute-start(bf16[2,96,768]{2,1,0:T(8,128)(2,1)S(1)} %pair_rows.3.refs_4_.refs_1_), channel_id=1, source_target_pairs={{0,16},{8,24},{16,0},{24,8},{1,17},{9,25},{17,1},{25,9},{2,18},{10... | collective-permute-start | bytes 884744 | tf_op jit(solution)/shard_map/ppermute | solution.py:37
  36.9 13.3 %collective-permute-start.7 = (bf16[2,96,768]{2,1,0:T(8,128)(2,1)}, bf16[2,96,768]{2,1,0:T(8,128)(2,1)}, u32[]{:S(2)}, u32[]{:S(2)}) collective-permute-start(bf16[2,96,768]{2,1,0:T(8,128)(2,1)} %pair_rows.4.refs_1_), channel_id=1, source_target_pairs={{0,4},{4,0},{1,5},{5,1},{2,6},{6,2},{3,7},{7,3},{8,12},{12,8},{9,1... | collective-permute-start | bytes 884744 | tf_op jit(solution)/shard_map/ppermute | solution.py:37
  54.0 19.4 %collective-permute-start.15 = (bf16[4,192,512]{2,1,0:T(8,128)(2,1)S(1)}, bf16[4,192,512]{2,1,0:T(8,128)(2,1)S(1)}, u32[]{:S(2)}, u32[]{:S(2)}) collective-permute-start(bf16[4,192,512]{2,1,0:T(8,128)(2,1)S(1)} %get-tuple-element.124.refs_1_.refs_4_), channel_id=1, source_target_pairs={{0,4},{4,0},{1,5},{5,1},{2,6},{6,2},{3,7},{7,3},{8,12},{12,8},{9,1... | collective-permute-start | bytes 2359304 | tf_op jit(solution)/shard_map/ppermute | solution.py:37
  81.7 28.1 %collective-permute-start.22 = (bf16[2,768,384]{2,1,0:T(8,128)(2,1)S(1)}, bf16[2,768,384]{2,1,0:T(8,128)(2,1)S(1)}, u32[]{:S(2)}, u32[]{:S(2)}) collective-permute-start(bf16[2,768,384]{2,1,0:T(8,128)(2,1)S(1)} %get-tuple-element.156), channel_id=1, source_target_pairs={{0,1},{1,0},{2,3},{3,2},{4,5},{5,4},{6,7},{7,6},{8,9},{9,8},{10,11... | collective-permute-start | bytes 3538952 | tf_op jit(solution)/shard_map/ppermute | solution.py:37
  86.3 23.5 %collective-permute-start.23 = (bf16[4,192,384]{2,1,0:T(8,128)(2,1)S(1)}, bf16[4,192,384]{2,1,0:T(8,128)(2,1)S(1)}, u32[]{:S(2)}, u32[]{:S(2)}) collective-permute-start(bf16[4,192,384]{2,1,0:T(8,128)(2,1)S(1)} %get-tuple-element.158), channel_id=1, source_target_pairs={{0,8},{8,0},{16,24},{24,16},{1,9},{9,1},{17,25},{25,17},{2,10},{10... | collective-permute-start | bytes 1769480 | tf_op jit(solution)/shard_map/ppermute | solution.py:37
  86.9 23.0 %collective-permute-start.24 = (bf16[4,192,384]{2,1,0:T(8,128)(2,1)S(1)}, bf16[4,192,384]{2,1,0:T(8,128)(2,1)S(1)}, u32[]{:S(2)}, u32[]{:S(2)}) collective-permute-start(bf16[4,192,384]{2,1,0:T(8,128)(2,1)S(1)} %get-tuple-element.160), channel_id=1, source_target_pairs={{0,16},{8,24},{16,0},{24,8},{1,17},{9,25},{17,1},{25,9},{2,18},{10... | collective-permute-start | bytes 1769480 | tf_op jit(solution)/shard_map/ppermute | solution.py:37
  104.5 10.6 %collective-permute-start.19 = (bf16[4,576,512]{2,1,0:T(8,128)(2,1)S(1)}, bf16[4,576,512]{2,1,0:T(8,128)(2,1)S(1)}, u32[]{:S(2)}, u32[]{:S(2)}) collective-permute-start(bf16[4,576,512]{2,1,0:T(8,128)(2,1)S(1)} %get-tuple-element.144.refs_0_), channel_id=1, source_target_pairs={{0,4},{4,0},{1,5},{5,1},{2,6},{6,2},{3,7},{7,3},{8,12},{12,8},{9,1... | collective-permute-start | bytes 7077896 | tf_op jit(solution)/shard_map/ppermute | solution.py:37
  111.1 16.3 %collective-permute-start.27 = (bf16[768,384]{1,0:T(8,128)(2,1)S(1)}, bf16[768,384]{1,0:T(8,128)(2,1)S(1)}, u32[]{:S(2)}, u32[]{:S(2)}) collective-permute-start(bf16[768,384]{1,0:T(8,128)(2,1)S(1)} %get-tuple-element.168), channel_id=1, source_target_pairs={{0,8},{8,0},{16,24},{24,16},{1,9},{9,1},{17,25},{25,17},{2,10},{10... | collective-permute-start | bytes 1769480 | tf_op jit(solution)/shard_map/ppermute | solution.py:37
  111.7 16.2 %collective-permute-start.28 = (bf16[768,384]{1,0:T(8,128)(2,1)S(1)}, bf16[768,384]{1,0:T(8,128)(2,1)S(1)}, u32[]{:S(2)}, u32[]{:S(2)}) collective-permute-start(bf16[768,384]{1,0:T(8,128)(2,1)S(1)} %get-tuple-element.170), channel_id=1, source_target_pairs={{0,16},{8,24},{16,0},{24,8},{1,17},{9,25},{17,1},{25,9},{2,18},{10... | collective-permute-start | bytes 1769480 | tf_op jit(solution)/shard_map/ppermute | solution.py:37
  119.1 20.9 %collective-permute-start.25 = (bf16[4,192,384]{2,1,0:T(8,128)(2,1)S(1)}, bf16[4,192,384]{2,1,0:T(8,128)(2,1)S(1)}, u32[]{:S(2)}, u32[]{:S(2)}) collective-permute-start(bf16[4,192,384]{2,1,0:T(8,128)(2,1)S(1)} %get-tuple-element.164), channel_id=1, source_target_pairs={{0,8},{8,0},{16,24},{24,16},{1,9},{9,1},{17,25},{25,17},{2,10},{10... | collective-permute-start | bytes 1769480 | tf_op jit(solution)/shard_map/ppermute | solution.py:37
  120.7 22.0 %collective-permute-start.26 = (bf16[4,224,384]{2,1,0:T(8,128)(2,1)S(1)}, bf16[4,224,384]{2,1,0:T(8,128)(2,1)S(1)}, u32[]{:S(2)}, u32[]{:S(2)}) collective-permute-start(bf16[4,224,384]{2,1,0:T(8,128)(2,1)S(1)} %get-tuple-element.166), channel_id=1, source_target_pairs={{0,16},{8,24},{16,0},{24,8},{1,17},{9,25},{17,1},{25,9},{2,18},{10... | collective-permute-start | bytes 2064392 | tf_op jit(solution)/shard_map/ppermute | solution.py:37
  128.8 17.5 %collective-permute-start.33 = (bf16[2,192,384]{2,1,0:T(8,128)(2,1)S(1)}, bf16[2,192,384]{2,1,0:T(8,128)(2,1)S(1)}, u32[]{:S(2)}, u32[]{:S(2)}) collective-permute-start(bf16[2,192,384]{2,1,0:T(8,128)(2,1)S(1)} %get-tuple-element.182), channel_id=1, source_target_pairs={{0,1},{1,0},{2,3},{3,2},{4,5},{5,4},{6,7},{7,6},{8,9},{9,8},{10,11... | collective-permute-start | bytes 884744 | tf_op jit(solution)/shard_map/ppermute | solution.py:37
  130.2 16.1 %collective-permute-start.31 = (bf16[2,96,384]{2,1,0:T(8,128)(2,1)S(1)}, bf16[2,96,384]{2,1,0:T(8,128)(2,1)S(1)}, u32[]{:S(2)}, u32[]{:S(2)}) collective-permute-start(bf16[2,96,384]{2,1,0:T(8,128)(2,1)S(1)} %get-tuple-element.178), channel_id=1, source_target_pairs={{0,8},{8,0},{16,24},{24,16},{1,9},{9,1},{17,25},{25,17},{2,10},{10... | collective-permute-start | bytes 442376 | tf_op jit(solution)/shard_map/ppermute | solution.py:37
  131.7 14.6 %collective-permute-start.32 = (bf16[2,96,384]{2,1,0:T(8,128)(2,1)S(1)}, bf16[2,96,384]{2,1,0:T(8,128)(2,1)S(1)}, u32[]{:S(2)}, u32[]{:S(2)}) collective-permute-start(bf16[2,96,384]{2,1,0:T(8,128)(2,1)S(1)} %get-tuple-element.180), channel_id=1, source_target_pairs={{0,16},{8,24},{16,0},{24,8},{1,17},{9,25},{17,1},{25,9},{2,18},{10... | collective-permute-start | bytes 442376 | tf_op jit(solution)/shard_map/ppermute | solution.py:37
  147.0 13.2 %collective-permute-start.35 = (bf16[384,384]{1,0:T(8,128)(2,1)S(1)}, bf16[384,384]{1,0:T(8,128)(2,1)S(1)}, u32[]{:S(2)}, u32[]{:S(2)}) collective-permute-start(bf16[384,384]{1,0:T(8,128)(2,1)S(1)} %get-tuple-element.188), channel_id=1, source_target_pairs={{0,2},{1,3},{2,0},{3,1},{4,6},{5,7},{6,4},{7,5},{8,10},{9,11},{10,... | collective-permute-start | bytes 884744 | tf_op jit(solution)/shard_map/ppermute | solution.py:37
  152.7 11.6 %collective-permute-start.34 = (bf16[2,208,384]{2,1,0:T(8,128)(2,1)S(1)}, bf16[2,208,384]{2,1,0:T(8,128)(2,1)S(1)}, u32[]{:S(2)}, u32[]{:S(2)}) collective-permute-start(bf16[2,208,384]{2,1,0:T(8,128)(2,1)S(1)} %get-tuple-element.186), channel_id=1, source_target_pairs={{0,1},{1,0},{2,3},{3,2},{4,5},{5,4},{6,7},{7,6},{8,9},{9,8},{10,11... | collective-permute-start | bytes 958472 | tf_op jit(solution)/shard_map/ppermute | solution.py:37
  160.8 13.1 %collective-permute-start.42 = (bf16[384,384]{1,0:T(8,128)(2,1)S(1)}, bf16[384,384]{1,0:T(8,128)(2,1)S(1)}, u32[]{:S(2)}, u32[]{:S(2)}) collective-permute-start(bf16[384,384]{1,0:T(8,128)(2,1)S(1)} %get-tuple-element.195.refs_0_), channel_id=1, source_target_pairs={{0,24},{8,16},{16,8},{24,0},{1,25},{9,17},{17,9},{25,1},{2,26},{10... | collective-permute-start | bytes 884744 | tf_op jit(solution)/shard_map/ppermute | solution.py:37
  162.4 13.6 %collective-permute-start.41 = (bf16[384,384]{1,0:T(8,128)(2,1)S(1)}, bf16[384,384]{1,0:T(8,128)(2,1)S(1)}, u32[]{:S(2)}, u32[]{:S(2)}) collective-permute-start(bf16[384,384]{1,0:T(8,128)(2,1)S(1)} %get-tuple-element.195.refs_0_), channel_id=1, source_target_pairs={{0,16},{8,24},{16,0},{24,8},{1,17},{9,25},{17,1},{25,9},{2,18},{10... | collective-permute-start | bytes 884744 | tf_op jit(solution)/shard_map/ppermute | solution.py:37
  162.7 13.3 %collective-permute-start.40 = (bf16[384,384]{1,0:T(8,128)(2,1)S(1)}, bf16[384,384]{1,0:T(8,128)(2,1)S(1)}, u32[]{:S(2)}, u32[]{:S(2)}) collective-permute-start(bf16[384,384]{1,0:T(8,128)(2,1)S(1)} %get-tuple-element.195.refs_0_), channel_id=1, source_target_pairs={{0,8},{8,0},{16,24},{24,16},{1,9},{9,1},{17,25},{25,17},{2,10},{10... | collective-permute-start | bytes 884744 | tf_op jit(solution)/shard_map/ppermute | solution.py:37
  (35 other events, 208.2 us)

commit v2 on v1

--- a/solution.py
+++ b/solution.py
@@ -860,17 +860,17 @@
     attn_held = fourth(*attn_held)
     attn_held = gather_back(fifth(*attn_held))
 
-    def both_cores(held):
+    def both_cores(held, macs=0):
         shape = (heads,) + held[0].shape
-        (pieces,) = run_whole(collect, places, held, [(shape, LOW)])
+        (pieces,) = run_whole(collect, places, held, [(shape, LOW)], macs=macs)
         return [(a, whole(shape)) for a in (pieces, swap_core(pieces))]
 
     ffn_held = both_cores(ffn_held)
+    attn_held = both_cores(attn_held, ffn_macs)
     outs = [(shape, F32, whole(shape)) for shape in ((chunk, width), (width, chunk))]
     grad_down, grad_up = run(
         ffn_place, places, (1,), ffn_held, outs, [pltpu.VMEM((width, chunk), F32)]
     )
-    attn_held = both_cores(attn_held)
     shapes = [
         (3, local_width, width),
         (local_width, width),

time: 193 us -> 190 us (0.984)
  waiting for transfers between devices: 64.9 us -> 61.1 us
    ppermute x45, waiting for transfers between devices: 64.9 us -> 61.1 us  [swap(): return lax.ppermute(value, axis, [(i, i ^ bit) for i in range(size)])]
  transfers between devices with their start and end apart: 45 -> 45, of which waited for: 21 -> 21; matrix products, arithmetic and copies ran while one was open for 1% -> 1% of each run, Pallas kernels for 39% -> 40%
where the time goes in v2:
time: 190 us
  Pallas kernels  82.2 us (43%)
  waiting for transfers between devices  61.1 us (32%)
  starting transfers between devices  41.7 us (22%)
    pallas_call x25, Pallas kernels, run_whole(): pl.pallas_call(body, name=getattr(kernel, 'func', kernel).__name__, in_sp...  72.3 us
    ppermute x45, waiting for transfers between devices, swap(): return lax.ppermute(value, axis, [(i, i ^ bit) for i in range(size)])  61.1 us
    ppermute x45, starting transfers between devices, swap(): return lax.ppermute(value, axis, [(i, i ^ bit) for i in range(size)])  41.7 us
    pallas_call x3, Pallas kernels, run(): pl.pallas_call(body, name=getattr(kernel, 'func', kernel).__name__, grid_...  9.88 us
  transfers between devices with their start and end apart: 45, of which 21 were waited for; matrix products, arithmetic and copies ran while one was open for 1% of the time, Pallas kernels for 40%

profile of v2, /device:TPU:0, one launch (start us, length us, event | category | flops | bytes accessed | tf_op | source)
XLA Modules:
  0.0 189.7 jit_solution(14211933409141604797)
XLA Ops:
  3.3 3.0 %collective-permute-start.4 = (bf16[112,768]{1,0:T(8,128)(2,1)}, bf16[112,768]{1,0:T(8,128)(2,1)}, u32[]{:S(2)}, u32[]{:S(2)}) collective-permute-start(bf16[112,768]{1,0:T(8,128)(2,1)} %pad_maximum_fusion.1), channel_id=1, source_target_pairs={{0,1},{1,0},{2,3},{3,2},{4,5},{5,4},{6,7},{7,6},{8,9},{9,8},{10,11... | collective-permute-start | bytes 516104 | tf_op jit(solution)/shard_map/ppermute | solution.py:37
  6.3 2.6 %collective-permute-start.2 = (bf16[112,768]{1,0:T(8,128)(2,1)}, bf16[112,768]{1,0:T(8,128)(2,1)S(1)}, u32[]{:S(2)}, u32[]{:S(2)}) collective-permute-start(bf16[112,768]{1,0:T(8,128)(2,1)} %pad_maximum_fusion.1), channel_id=1, source_target_pairs={{0,2},{1,3},{2,0},{3,1},{4,6},{5,7},{6,4},{7,5},{8,10},{9,11},{10,... | collective-permute-start | bytes 516104 | tf_op jit(solution)/shard_map/ppermute | solution.py:37
  9.0 4.7 %collective-permute-done.4.refs_0_.refs_5_ = bf16[112,768]{1,0:T(8,128)(2,1)} collective-permute-done((bf16[112,768]{1,0:T(8,128)(2,1)}, bf16[112,768]{1,0:T(8,128)(2,1)}, u32[]{:S(2)}, u32[]{:S(2)}) %collective-permute-start.4) | collective-permute-done | bytes 172064 | tf_op jit(solution)/shard_map/ppermute | solution.py:37
  16.4 5.7 %collective-permute-done.2.refs_2_.refs_0_.refs_5_ = bf16[112,768]{1,0:T(8,128)(2,1)S(1)} collective-permute-done((bf16[112,768]{1,0:T(8,128)(2,1)}, bf16[112,768]{1,0:T(8,128)(2,1)S(1)}, u32[]{:S(2)}, u32[]{:S(2)}) %collective-permute-start.2) | collective-permute-done | bytes 172064 | tf_op jit(solution)/shard_map/ppermute | solution.py:37
  26.7 2.9 %own_attention.1 = (bf16[4,576,512]{2,1,0:T(8,128)(2,1)S(1)}, bf16[4,192,512]{2,1,0:T(8,128)(2,1)S(1)}, f32[4,8,512]{2,1,0:T(8,128)S(1)}, bf16[4,576,768]{2,1,0:T(8,128)(2,1)S(1)}, bf16[4,192,768]{2,1,0:T(8,128)(2,1)S(1)}) custom-call(s32[3]{0:T(128)S(1)} %pad_add_fusion.places, bf16[512,768]{1,0:T(8,128)(2,1)S(1)} %constant_dynamic-slice_fusion.refs_0_.refs_2_, ...), custom_call_target="tpu_custom_call" | custom-call | flops 10066329600 | tf_op jit(solution)/shard_map/own_attention/pallas_call | solution.py:135
  31.2 4.4 %collective-permute-done.8.refs_2_ = bf16[2,96,768]{2,1,0:T(8,128)(2,1)S(1)} collective-permute-done((bf16[2,96,768]{2,1,0:T(8,128)(2,1)S(1)}, bf16[2,96,768]{2,1,0:T(8,128)(2,1)S(1)}, u32[]{:S(2)}, u32[]{:S(2)}) %collective-permute-start.8) | collective-permute-done | bytes 294944 | tf_op jit(solution)/shard_map/ppermute | solution.py:37
  39.4 3.4 %far_attention.3 = (bf16[4,576,512]{2,1,0:T(8,128)(2,1)S(1)}, bf16[4,192,512]{2,1,0:T(8,128)(2,1)S(1)}, f32[4,8,512]{2,1,0:T(8,128)S(1)}, bf16[4,576,768]{2,1,0:T(8,128)(2,1)S(1)}, bf16[4,192,768]{2,1,0:T(8,128)(2,1)S(1)}) custom-call(s32[3]{0:T(128)S(1)} %pad_add_fusion.places, ...), custom_call_target="tpu_custom_call", output_to_operand_aliasing={{0}: (8, {}), {1}: (9, {}), {2}: (10, {}), {3}: (11, {}), {... | custom-call | flops 125829120000 | tf_op jit(solution)/shard_map/far_attention/pallas_call | solution.py:135
  42.8 3.7 %collective-permute-done.6.refs_0_.refs_2_ = bf16[2,96,768]{2,1,0:T(8,128)(2,1)S(1)} collective-permute-done((bf16[2,96,768]{2,1,0:T(8,128)(2,1)}, bf16[2,96,768]{2,1,0:T(8,128)(2,1)S(1)}, u32[]{:S(2)}, u32[]{:S(2)}) %collective-permute-start.6) | collective-permute-done | bytes 294944 | tf_op jit(solution)/shard_map/ppermute | solution.py:37
  47.2 3.0 %far_attention.4 = (bf16[4,576,512]{2,1,0:T(8,128)(2,1)S(1)}, bf16[4,192,512]{2,1,0:T(8,128)(2,1)S(1)}, f32[4,8,512]{2,1,0:T(8,128)S(1)}, bf16[4,576,768]{2,1,0:T(8,128)(2,1)S(1)}, bf16[4,192,768]{2,1,0:T(8,128)(2,1)S(1)}) custom-call(s32[3]{0:T(128)S(1)} %pad_add_fusion.places, ...), custom_call_target="tpu_custom_call", output_to_operand_aliasing={{0}: (8, {}), {1}: (9, {}), {2}: (10, {}), {3}: (11, {}), {... | custom-call | flops 125829120000 | tf_op jit(solution)/shard_map/far_attention/pallas_call | solution.py:135
  50.3 3.7 %far_attention.5 = (bf16[4,576,512]{2,1,0:T(8,128)(2,1)S(1)}, bf16[4,192,512]{2,1,0:T(8,128)(2,1)S(1)}, f32[4,8,512]{2,1,0:T(8,128)S(1)}, bf16[4,576,768]{2,1,0:T(8,128)(2,1)S(1)}, bf16[4,192,768]{2,1,0:T(8,128)(2,1)S(1)}) custom-call(s32[3]{0:T(128)S(1)} %pad_add_fusion.places, ...), custom_call_target="tpu_custom_call", output_to_operand_aliasing={{0}: (8, {}), {1}: (9, {}), {2}: (10, {}), {3}: (11, {}), {... | custom-call | flops 125829120000 | tf_op jit(solution)/shard_map/far_attention/pallas_call | solution.py:135
  54.6 18.2 %feed_forward.1 = (bf16[4,512,384]{2,1,0:T(8,128)(2,1)S(1)}, bf16[4,512,384]{2,1,0:T(8,128)(2,1)S(1)}, bf16[4,512,384]{2,1,0:T(8,128)(2,1)S(1)}, bf16[4,512,768]...) custom-call(s32[3]{0:T(128)S(1)} %pad_add_fusion.places, ...), custom_call_target="tpu_custom_call" | custom-call | flops 38654705664 | tf_op jit(solution)/shard_map/feed_forward/pallas_call | solution.py:135
  73.4 3.7 %inner_back.1 = (bf16[4,512,384]{2,1,0:T(8,128)(2,1)S(1)}, bf16[4,512,384]{2,1,0:T(8,128)(2,1)S(1)}, f32[4,1,768]{2,1,0:T(1,128)S(1)}, f32[8,128]{1,0:T(8,128)S(1)}) custom-call(s32[3]{0:T(128)S(1)} %pad_add_fusion.places, bf16[4,512,384]{2,1,0:T(8,128)(2,1)S(1)} %get-tuple-element.128.refs_0_.refs_2_, bf16[3072,768]{1,0:T(8,128)(2,1)S(1)} %copy-done.4, ...), custom_call_target="tpu_custom_call" | custom-call | flops 19327352832 | tf_op jit(solution)/shard_map/inner_back/pallas_call | solution.py:135
  78.5 3.2 %down_grad.1 = (bf16[2,768,384]{2,1,0:T(8,128)(2,1)S(1)}, bf16[2,768,384]{2,1,0:T(8,128)(2,1)S(1)}, f32[8,128]{1,0:T(8,128)S(1)}) custom-call(s32[3]{0:T(128)S(1)} %pad_add_fusion.places, bf16[4,512,384]{2,1,0:T(8,128)(2,1)S(1)} %get-tuple-element.136.refs_0_, bf16[4,512,384]{2,1,0:T(8,128)(2,1)S(1)} %collective-permute-done.18.refs_1_, ...), custom_call_target="tpu_custom_call" | custom-call | flops 19327352832 | tf_op jit(solution)/shard_map/down_grad/pallas_call | solution.py:135
  83.1 3.2 %up_grad.1 = (bf16[4,192,384]{2,1,0:T(8,128)(2,1)S(1)}, bf16[4,192,384]{2,1,0:T(8,128)(2,1)S(1)}, bf16[4,192,384]{2,1,0:T(8,128)(2,1)S(1)}, bf16[4,192,384]{2,1,0:T(8,128)(2,1)S(1)}, f32[8,128]{1,0:T(8,128)S(1)}) custom-call(s32[3]{0:T(128)S(1)} %pad_add_fusion.places, bf16[4,512,384]{2,1,0:T(8,128)(2,1)S(1)} %get-tuple-element.131.refs_0_, ...), custom_call_target="tpu_custom_call" | custom-call | flops 24159192 | tf_op jit(solution)/shard_map/up_grad/pallas_call | solution.py:135
  88.4 4.2 %hidden_back.1 = (bf16[512,384]{1,0:T(8,128)(2,1)S(1)}, f32[512,768]{1,0:T(8,128)S(1)}, bf16[512,768]{1,0:T(8,128)(2,1)S(1)}, f32[8,768]{1,0:T(8,128)S(1)}, f32[8,128]{1,0:T(8,128)S(1)}) custom-call(s32[3]{0:T(128)S(1)} %pad_add_fusion.places, bf16[4,512,384]{2,1,0:T(8,128)(2,1)S(1)} %get-tuple-element.131.refs_0_, ...), custom_call_target="tpu_custom_call" | custom-call | flops 24159192 | tf_op jit(solution)/shard_map/hidden_back/pallas_call | solution.py:135
  92.6 11.8 %attention_back.1 = (bf16[4,576,512]{2,1,0:T(8,128)(2,1)S(1)}, f32[4,8,576]{2,1,0:T(8,128)S(1)}, f32[8,128]{1,0:T(8,128)S(1)}) custom-call(s32[3]{0:T(128)S(1)} %pad_add_fusion.places, bf16[4,576,512]{2,1,0:T(8,128)(2,1)S(1)} %get-tuple-element.127.refs_0_, bf16[4,192,768]{2,1,0:T(8,128)(2,1)S(1)} %get-tuple-element.125.refs_2_.refs_1_, ...), custom_call_target="tpu_custom_call" | custom-call | tf_op jit(solution)/shard_map/attention_back/pallas_call | solution.py:135
  104.6 3.8 %input_sum.1 = (f32[512,768]{1,0:T(8,128)}, f32[8,128]{1,0:T(8,128)S(1)}) custom-call(s32[3]{0:T(128)S(1)} %pad_add_fusion.places, bf16[4,576,512]{2,1,0:T(8,128)(2,1)S(1)} %get-tuple-element.144.refs_0_, bf16[4,576,768]{2,1,0:T(8,128)(2,1)S(1)} %get-tuple-element.145.refs_1_, f32[512,768]{1,0:T(8,128)S(1)} %get-tuple-element.146.refs_2_, ...), custom_call_target="tpu_custom_call" | custom-call | bytes 90439 | tf_op jit(solution)/shard_map/input_sum/pallas_call | solution.py:92
  115.1 4.0 %attn_grad.1 = (bf16[4,192,384]{2,1,0:T(8,128)(2,1)S(1)}, bf16[4,192,384]{2,1,0:T(8,128)(2,1)S(1)}, bf16[4,224,384]{2,1,0:T(8,128)(2,1)S(1)}, bf16[4,224,384]{2,1,0:T(8,128)(2,1)S(1)}, f32[8,128]{1,0:T(8,128)S(1)}) custom-call(s32[3]{0:T(128)S(1)} %pad_add_fusion.places, bf16[4,576,512]{2,1,0:T(8,128)(2,1)S(1)} %get-tuple-element.144.refs_0_, ...), custom_call_target="tpu_custom_call" | custom-call | tf_op jit(solution)/shard_map/attn_grad/pallas_call | solution.py:135
  121.6 5.8 %collective-permute-done.27.refs_1_ = bf16[768,384]{1,0:T(8,128)(2,1)S(1)} collective-permute-done((bf16[768,384]{1,0:T(8,128)(2,1)S(1)}, bf16[768,384]{1,0:T(8,128)(2,1)S(1)}, u32[]{:S(2)}, u32[]{:S(2)}) %collective-permute-start.27) | collective-permute-done | bytes 589856 | tf_op jit(solution)/shard_map/ppermute | solution.py:37
  133.2 6.7 %collective-permute-done.25.refs_1_ = bf16[4,192,384]{2,1,0:T(8,128)(2,1)S(1)} collective-permute-done((bf16[4,192,384]{2,1,0:T(8,128)(2,1)S(1)}, bf16[4,192,384]{2,1,0:T(8,128)(2,1)S(1)}, u32[]{:S(2)}, u32[]{:S(2)}) %collective-permute-start.25) | collective-permute-done | bytes 589856 | tf_op jit(solution)/shard_map/ppermute | solution.py:37
  140.0 2.7 %collective-permute-done.26.refs_3_ = bf16[4,224,384]{2,1,0:T(8,128)(2,1)S(1)} collective-permute-done((bf16[4,224,384]{2,1,0:T(8,128)(2,1)S(1)}, bf16[4,224,384]{2,1,0:T(8,128)(2,1)S(1)}, u32[]{:S(2)}, u32[]{:S(2)}) %collective-permute-start.26) | collective-permute-done | bytes 688160 | tf_op jit(solution)/shard_map/ppermute | solution.py:37
  154.2 5.9 %collective-permute-done.35.refs_1_ = bf16[384,384]{1,0:T(8,128)(2,1)S(1)} collective-permute-done((bf16[384,384]{1,0:T(8,128)(2,1)S(1)}, bf16[384,384]{1,0:T(8,128)(2,1)S(1)}, u32[]{:S(2)}, u32[]{:S(2)}) %collective-permute-start.35) | collective-permute-done | bytes 294944 | tf_op jit(solution)/shard_map/ppermute | solution.py:37
  167.1 5.5 %collective-permute-done.36.refs_1_ = bf16[208,384]{1,0:T(8,128)(2,1)S(1)} collective-permute-done((bf16[208,384]{1,0:T(8,128)(2,1)S(1)}, bf16[208,384]{1,0:T(8,128)(2,1)S(1)}, u32[]{:S(2)}, u32[]{:S(2)}) %collective-permute-start.36) | collective-permute-done | bytes 159776 | tf_op jit(solution)/shard_map/ppermute | solution.py:37
  183.6 3.8 %ffn_place.1 = (f32[768,768]{1,0:T(8,128)}, f32[768,768]{1,0:T(8,128)}, f32[8,128]{1,0:T(8,128)S(1)}) custom-call(s32[3]{0:T(128)S(1)} %pad_add_fusion.places, bf16[4,384,384]{2,1,0:T(8,128)(2,1)S(1)} %get-tuple-element.199.refs_0_, bf16[4,384,384]{2,1,0:T(8,128)(2,1)S(1)} %collective-permute-done.44.refs_1_, f32[8,128]{1,0:T(8,128)S(1)} %get-tuple-element.200.refs_2_), custom_call_target="tpu_custom_call" | custom-call | bytes 56623104 | tf_op jit(solution)/shard_map/ffn_place/pallas_call | solution.py:92
  (131 shorter events, 68.8 us)
Async XLA Ops:
  3.3 10.4 %collective-permute-start.4 = (bf16[112,768]{1,0:T(8,128)(2,1)}, bf16[112,768]{1,0:T(8,128)(2,1)}, u32[]{:S(2)}, u32[]{:S(2)}) collective-permute-start(bf16[112,768]{1,0:T(8,128)(2,1)} %pad_maximum_fusion.1), channel_id=1, source_target_pairs={{0,1},{1,0},{2,3},{3,2},{4,5},{5,4},{6,7},{7,6},{8,9},{9,8},{10,11... | collective-permute-start | bytes 516104 | tf_op jit(solution)/shard_map/ppermute | solution.py:37
  6.3 15.8 %collective-permute-start.2 = (bf16[112,768]{1,0:T(8,128)(2,1)}, bf16[112,768]{1,0:T(8,128)(2,1)S(1)}, u32[]{:S(2)}, u32[]{:S(2)}) collective-permute-start(bf16[112,768]{1,0:T(8,128)(2,1)} %pad_maximum_fusion.1), channel_id=1, source_target_pairs={{0,2},{1,3},{2,0},{3,1},{4,6},{5,7},{6,4},{7,5},{8,10},{9,11},{10,... | collective-permute-start | bytes 516104 | tf_op jit(solution)/shard_map/ppermute | solution.py:37
  8.9 14.7 %collective-permute-start = (bf16[112,768]{1,0:T(8,128)(2,1)}, bf16[112,768]{1,0:T(8,128)(2,1)S(1)}, u32[]{:S(2)}, u32[]{:S(2)}) collective-permute-start(bf16[112,768]{1,0:T(8,128)(2,1)} %pad_maximum_fusion.1), channel_id=1, source_target_pairs={{0,3},{1,2},{2,1},{3,0},{4,7},{5,6},{6,5},{7,4},{8,11},{9,10},{10,... | collective-permute-start | bytes 516104 | tf_op jit(solution)/shard_map/ppermute | solution.py:37
  13.7 11.4 %collective-permute-start.5 = (bf16[112,768]{1,0:T(8,128)(2,1)}, bf16[112,768]{1,0:T(8,128)(2,1)S(1)}, u32[]{:S(2)}, u32[]{:S(2)}) collective-permute-start(bf16[112,768]{1,0:T(8,128)(2,1)} %collective-permute-done.4.refs_0_.refs_5_), channel_id=1, source_target_pairs={{0,8},{8,0},{16,24},{24,16},{1,9},{9,1},{17,25},{25,17},{2,10},{10... | collective-permute-start | bytes 516104 | tf_op jit(solution)/shard_map/ppermute | solution.py:37
  26.1 11.8 %collective-permute-start.9 = (bf16[2,96,768]{2,1,0:T(8,128)(2,1)S(1)}, bf16[2,96,768]{2,1,0:T(8,128)(2,1)S(1)}, u32[]{:S(2)}, u32[]{:S(2)}) collective-permute-start(bf16[2,96,768]{2,1,0:T(8,128)(2,1)S(1)} %pair_rows.3.refs_4_.refs_1_), channel_id=1, source_target_pairs={{0,4},{4,0},{1,5},{5,1},{2,6},{6,2},{3,7},{7,3},{8,12},{12,8},{9,1... | collective-permute-start | bytes 884744 | tf_op jit(solution)/shard_map/ppermute | solution.py:37
  26.2 9.4 %collective-permute-start.8 = (bf16[2,96,768]{2,1,0:T(8,128)(2,1)S(1)}, bf16[2,96,768]{2,1,0:T(8,128)(2,1)S(1)}, u32[]{:S(2)}, u32[]{:S(2)}) collective-permute-start(bf16[2,96,768]{2,1,0:T(8,128)(2,1)S(1)} %pair_rows.3.refs_4_.refs_1_), channel_id=1, source_target_pairs={{0,16},{8,24},{16,0},{24,8},{1,17},{9,25},{17,1},{25,9},{2,18},{10... | collective-permute-start | bytes 884744 | tf_op jit(solution)/shard_map/ppermute | solution.py:37
  36.9 13.3 %collective-permute-start.7 = (bf16[2,96,768]{2,1,0:T(8,128)(2,1)}, bf16[2,96,768]{2,1,0:T(8,128)(2,1)}, u32[]{:S(2)}, u32[]{:S(2)}) collective-permute-start(bf16[2,96,768]{2,1,0:T(8,128)(2,1)} %pair_rows.4.refs_1_), channel_id=1, source_target_pairs={{0,4},{4,0},{1,5},{5,1},{2,6},{6,2},{3,7},{7,3},{8,12},{12,8},{9,1... | collective-permute-start | bytes 884744 | tf_op jit(solution)/shard_map/ppermute | solution.py:37
  54.0 19.4 %collective-permute-start.15 = (bf16[4,192,512]{2,1,0:T(8,128)(2,1)S(1)}, bf16[4,192,512]{2,1,0:T(8,128)(2,1)S(1)}, u32[]{:S(2)}, u32[]{:S(2)}) collective-permute-start(bf16[4,192,512]{2,1,0:T(8,128)(2,1)S(1)} %get-tuple-element.124.refs_1_.refs_4_), channel_id=1, source_target_pairs={{0,4},{4,0},{1,5},{5,1},{2,6},{6,2},{3,7},{7,3},{8,12},{12,8},{9,1... | collective-permute-start | bytes 2359304 | tf_op jit(solution)/shard_map/ppermute | solution.py:37
  81.7 28.1 %collective-permute-start.22 = (bf16[2,768,384]{2,1,0:T(8,128)(2,1)S(1)}, bf16[2,768,384]{2,1,0:T(8,128)(2,1)S(1)}, u32[]{:S(2)}, u32[]{:S(2)}) collective-permute-start(bf16[2,768,384]{2,1,0:T(8,128)(2,1)S(1)} %get-tuple-element.156), channel_id=1, source_target_pairs={{0,1},{1,0},{2,3},{3,2},{4,5},{5,4},{6,7},{7,6},{8,9},{9,8},{10,11... | collective-permute-start | bytes 3538952 | tf_op jit(solution)/shard_map/ppermute | solution.py:37
  86.3 23.5 %collective-permute-start.23 = (bf16[4,192,384]{2,1,0:T(8,128)(2,1)S(1)}, bf16[4,192,384]{2,1,0:T(8,128)(2,1)S(1)}, u32[]{:S(2)}, u32[]{:S(2)}) collective-permute-start(bf16[4,192,384]{2,1,0:T(8,128)(2,1)S(1)} %get-tuple-element.158), channel_id=1, source_target_pairs={{0,8},{8,0},{16,24},{24,16},{1,9},{9,1},{17,25},{25,17},{2,10},{10... | collective-permute-start | bytes 1769480 | tf_op jit(solution)/shard_map/ppermute | solution.py:37
  86.9 23.0 %collective-permute-start.24 = (bf16[4,192,384]{2,1,0:T(8,128)(2,1)S(1)}, bf16[4,192,384]{2,1,0:T(8,128)(2,1)S(1)}, u32[]{:S(2)}, u32[]{:S(2)}) collective-permute-start(bf16[4,192,384]{2,1,0:T(8,128)(2,1)S(1)} %get-tuple-element.160), channel_id=1, source_target_pairs={{0,16},{8,24},{16,0},{24,8},{1,17},{9,25},{17,1},{25,9},{2,18},{10... | collective-permute-start | bytes 1769480 | tf_op jit(solution)/shard_map/ppermute | solution.py:37
  104.5 10.6 %collective-permute-start.19 = (bf16[4,576,512]{2,1,0:T(8,128)(2,1)S(1)}, bf16[4,576,512]{2,1,0:T(8,128)(2,1)S(1)}, u32[]{:S(2)}, u32[]{:S(2)}) collective-permute-start(bf16[4,576,512]{2,1,0:T(8,128)(2,1)S(1)} %get-tuple-element.144.refs_0_), channel_id=1, source_target_pairs={{0,4},{4,0},{1,5},{5,1},{2,6},{6,2},{3,7},{7,3},{8,12},{12,8},{9,1... | collective-permute-start | bytes 7077896 | tf_op jit(solution)/shard_map/ppermute | solution.py:37
  111.1 16.3 %collective-permute-start.27 = (bf16[768,384]{1,0:T(8,128)(2,1)S(1)}, bf16[768,384]{1,0:T(8,128)(2,1)S(1)}, u32[]{:S(2)}, u32[]{:S(2)}) collective-permute-start(bf16[768,384]{1,0:T(8,128)(2,1)S(1)} %get-tuple-element.168), channel_id=1, source_target_pairs={{0,8},{8,0},{16,24},{24,16},{1,9},{9,1},{17,25},{25,17},{2,10},{10... | collective-permute-start | bytes 1769480 | tf_op jit(solution)/shard_map/ppermute | solution.py:37
  111.7 16.2 %collective-permute-start.28 = (bf16[768,384]{1,0:T(8,128)(2,1)S(1)}, bf16[768,384]{1,0:T(8,128)(2,1)S(1)}, u32[]{:S(2)}, u32[]{:S(2)}) collective-permute-start(bf16[768,384]{1,0:T(8,128)(2,1)S(1)} %get-tuple-element.170), channel_id=1, source_target_pairs={{0,16},{8,24},{16,0},{24,8},{1,17},{9,25},{17,1},{25,9},{2,18},{10... | collective-permute-start | bytes 1769480 | tf_op jit(solution)/shard_map/ppermute | solution.py:37
  119.1 20.9 %collective-permute-start.25 = (bf16[4,192,384]{2,1,0:T(8,128)(2,1)S(1)}, bf16[4,192,384]{2,1,0:T(8,128)(2,1)S(1)}, u32[]{:S(2)}, u32[]{:S(2)}) collective-permute-start(bf16[4,192,384]{2,1,0:T(8,128)(2,1)S(1)} %get-tuple-element.164), channel_id=1, source_target_pairs={{0,8},{8,0},{16,24},{24,16},{1,9},{9,1},{17,25},{25,17},{2,10},{10... | collective-permute-start | bytes 1769480 | tf_op jit(solution)/shard_map/ppermute | solution.py:37
  120.7 22.0 %collective-permute-start.26 = (bf16[4,224,384]{2,1,0:T(8,128)(2,1)S(1)}, bf16[4,224,384]{2,1,0:T(8,128)(2,1)S(1)}, u32[]{:S(2)}, u32[]{:S(2)}) collective-permute-start(bf16[4,224,384]{2,1,0:T(8,128)(2,1)S(1)} %get-tuple-element.166), channel_id=1, source_target_pairs={{0,16},{8,24},{16,0},{24,8},{1,17},{9,25},{17,1},{25,9},{2,18},{10... | collective-permute-start | bytes 2064392 | tf_op jit(solution)/shard_map/ppermute | solution.py:37
  128.8 17.5 %collective-permute-start.33 = (bf16[2,192,384]{2,1,0:T(8,128)(2,1)S(1)}, bf16[2,192,384]{2,1,0:T(8,128)(2,1)S(1)}, u32[]{:S(2)}, u32[]{:S(2)}) collective-permute-start(bf16[2,192,384]{2,1,0:T(8,128)(2,1)S(1)} %get-tuple-element.182), channel_id=1, source_target_pairs={{0,1},{1,0},{2,3},{3,2},{4,5},{5,4},{6,7},{7,6},{8,9},{9,8},{10,11... | collective-permute-start | bytes 884744 | tf_op jit(solution)/shard_map/ppermute | solution.py:37
  130.2 16.1 %collective-permute-start.31 = (bf16[2,96,384]{2,1,0:T(8,128)(2,1)S(1)}, bf16[2,96,384]{2,1,0:T(8,128)(2,1)S(1)}, u32[]{:S(2)}, u32[]{:S(2)}) collective-permute-start(bf16[2,96,384]{2,1,0:T(8,128)(2,1)S(1)} %get-tuple-element.178), channel_id=1, source_target_pairs={{0,8},{8,0},{16,24},{24,16},{1,9},{9,1},{17,25},{25,17},{2,10},{10... | collective-permute-start | bytes 442376 | tf_op jit(solution)/shard_map/ppermute | solution.py:37
  131.7 14.6 %collective-permute-start.32 = (bf16[2,96,384]{2,1,0:T(8,128)(2,1)S(1)}, bf16[2,96,384]{2,1,0:T(8,128)(2,1)S(1)}, u32[]{:S(2)}, u32[]{:S(2)}) collective-permute-start(bf16[2,96,384]{2,1,0:T(8,128)(2,1)S(1)} %get-tuple-element.180), channel_id=1, source_target_pairs={{0,16},{8,24},{16,0},{24,8},{1,17},{9,25},{17,1},{25,9},{2,18},{10... | collective-permute-start | bytes 442376 | tf_op jit(solution)/shard_map/ppermute | solution.py:37
  147.0 13.2 %collective-permute-start.35 = (bf16[384,384]{1,0:T(8,128)(2,1)S(1)}, bf16[384,384]{1,0:T(8,128)(2,1)S(1)}, u32[]{:S(2)}, u32[]{:S(2)}) collective-permute-start(bf16[384,384]{1,0:T(8,128)(2,1)S(1)} %get-tuple-element.188), channel_id=1, source_target_pairs={{0,2},{1,3},{2,0},{3,1},{4,6},{5,7},{6,4},{7,5},{8,10},{9,11},{10,... | collective-permute-start | bytes 884744 | tf_op jit(solution)/shard_map/ppermute | solution.py:37
  152.7 11.0 %collective-permute-start.34 = (bf16[2,208,384]{2,1,0:T(8,128)(2,1)S(1)}, bf16[2,208,384]{2,1,0:T(8,128)(2,1)S(1)}, u32[]{:S(2)}, u32[]{:S(2)}) collective-permute-start(bf16[2,208,384]{2,1,0:T(8,128)(2,1)S(1)} %get-tuple-element.186), channel_id=1, source_target_pairs={{0,1},{1,0},{2,3},{3,2},{4,5},{5,4},{6,7},{7,6},{8,9},{9,8},{10,11... | collective-permute-start | bytes 958472 | tf_op jit(solution)/shard_map/ppermute | solution.py:37
  160.8 14.1 %collective-permute-start.42 = (bf16[384,384]{1,0:T(8,128)(2,1)S(1)}, bf16[384,384]{1,0:T(8,128)(2,1)S(1)}, u32[]{:S(2)}, u32[]{:S(2)}) collective-permute-start(bf16[384,384]{1,0:T(8,128)(2,1)S(1)} %get-tuple-element.195.refs_0_), channel_id=1, source_target_pairs={{0,24},{8,16},{16,8},{24,0},{1,25},{9,17},{17,9},{25,1},{2,26},{10... | collective-permute-start | bytes 884744 | tf_op jit(solution)/shard_map/ppermute | solution.py:37
  164.9 13.7 %collective-permute-start.41 = (bf16[384,384]{1,0:T(8,128)(2,1)S(1)}, bf16[384,384]{1,0:T(8,128)(2,1)S(1)}, u32[]{:S(2)}, u32[]{:S(2)}) collective-permute-start(bf16[384,384]{1,0:T(8,128)(2,1)S(1)} %get-tuple-element.195.refs_0_), channel_id=1, source_target_pairs={{0,16},{8,24},{16,0},{24,8},{1,17},{9,25},{17,1},{25,9},{2,18},{10... | collective-permute-start | bytes 884744 | tf_op jit(solution)/shard_map/ppermute | solution.py:37
  165.6 13.0 %collective-permute-start.40 = (bf16[384,384]{1,0:T(8,128)(2,1)S(1)}, bf16[384,384]{1,0:T(8,128)(2,1)S(1)}, u32[]{:S(2)}, u32[]{:S(2)}) collective-permute-start(bf16[384,384]{1,0:T(8,128)(2,1)S(1)} %get-tuple-element.195.refs_0_), channel_id=1, source_target_pairs={{0,8},{8,0},{16,24},{24,16},{1,9},{9,1},{17,25},{25,17},{2,10},{10... | collective-permute-start | bytes 884744 | tf_op jit(solution)/shard_map/ppermute | solution.py:37
  (35 other events, 203.4 us)

commit v3 on v2

--- a/solution.py
+++ b/solution.py
@@ -248,8 +248,10 @@
     )
 
 
-def copy_rows(places, rows, out):
-    out[...] = rows[...]
+def copy_rows(places, *refs):
+    count = len(refs) // 2
+    for rows, out in zip(refs[:count], refs[count:]):
+        out[...] = rows[...]
 
 
 def pair_rows(places, first, second, out):
@@ -701,7 +703,7 @@
     ]
     macs = rows3 * width * own_rows + 6 * own_rows * own_rows * 256
     orders = [(1, 2) if d % 2 else (2, 1) for d in range(heads)]
-    nexts = [swap(first_hop[d - 1], "near", orders[d][0]) for d in range(1, heads)]
+    nexts = [swap(first_hop[0], "near", orders[1][0])]
 
     def pair_up(d, after):
         (pair,) = run_whole(
@@ -710,11 +712,15 @@
         )
         return pair
 
-    pairs = [pair_up(1, first_hop[1:])]
+    pairs = [pair_up(1, [])]
     ins = [tok_own, shard, bias, seg[None]]
     made = run_whole(
         own_attention, places, ins, attend_outs, macs=macs, after=pairs, chain=False
     )
+    late = run_whole(
+        copy_rows, places, first_hop[1:], [(piece.shape, LOW)] * 2, after=[made[2]], chain=False
+    )
+    nexts += [swap(late[d - 2], "near", orders[d][0]) for d in range(2, heads)]
     pairs += [pair_up(d, nexts[1:] + [made[2]]) for d in range(2, heads)]
     rests = [swap(pairs[d - 1], "near", orders[d][1]) for d in range(1, heads)]
     for d in range(1, heads):

time: 190 us -> 188 us (0.989)
  starting transfers between devices: 41.7 us -> 37.3 us
    ppermute x45, starting transfers between devices: 41.7 us -> 37.3 us  [swap(): return lax.ppermute(value, axis, [(i, i ^ bit) for i in range(size)])]
    pallas_call x25 -> x26, Pallas kernels: 72.3 us -> 73 us  [run_whole(): pl.pallas_call(body, name=getattr(kernel, 'func', kernel).__name__, in_sp...]
  transfers between devices with their start and end apart: 45 -> 45, of which waited for: 21 -> 23; matrix products, arithmetic and copies ran while one was open for 1% -> 1% of each run, Pallas kernels for 40% -> 41%
where the time goes in v3:
time: 188 us
  Pallas kernels  82.9 us (44%)
  waiting for transfers between devices  63 us (34%)
  starting transfers between devices  37.3 us (20%)
    pallas_call x26, Pallas kernels, run_whole(): pl.pallas_call(body, name=getattr(kernel, 'func', kernel).__name__, in_sp...  73 us
    ppermute x45, waiting for transfers between devices, swap(): return lax.ppermute(value, axis, [(i, i ^ bit) for i in range(size)])  63 us
    ppermute x45, starting transfers between devices, swap(): return lax.ppermute(value, axis, [(i, i ^ bit) for i in range(size)])  37.3 us
    pallas_call x3, Pallas kernels, run(): pl.pallas_call(body, name=getattr(kernel, 'func', kernel).__name__, grid_...  9.9 us
  transfers between devices with their start and end apart: 45, of which 23 were waited for; matrix products, arithmetic and copies ran while one was open for 1% of the time, Pallas kernels for 41%

profile of v3, /device:TPU:0, one launch (start us, length us, event | category | flops | bytes accessed | tf_op | source)
XLA Modules:
  0.0 188.0 jit_solution(15943930723502498787)
XLA Ops:
  3.3 3.0 %collective-permute-start.2 = (bf16[112,768]{1,0:T(8,128)(2,1)}, bf16[112,768]{1,0:T(8,128)(2,1)}, u32[]{:S(2)}, u32[]{:S(2)}) collective-permute-start(bf16[112,768]{1,0:T(8,128)(2,1)} %pad_maximum_fusion.1), channel_id=1, source_target_pairs={{0,1},{1,0},{2,3},{3,2},{4,5},{5,4},{6,7},{7,6},{8,9},{9,8},{10,11... | collective-permute-start | bytes 516104 | tf_op jit(solution)/shard_map/ppermute | solution.py:37
  9.0 4.7 %collective-permute-done.2.refs_0_.refs_5_ = bf16[112,768]{1,0:T(8,128)(2,1)} collective-permute-done((bf16[112,768]{1,0:T(8,128)(2,1)}, bf16[112,768]{1,0:T(8,128)(2,1)}, u32[]{:S(2)}, u32[]{:S(2)}) %collective-permute-start.2) | collective-permute-done | bytes 172064 | tf_op jit(solution)/shard_map/ppermute | solution.py:37
  16.4 3.0 %collective-permute-done.3.refs_1_ = bf16[112,768]{1,0:T(8,128)(2,1)S(1)} collective-permute-done((bf16[112,768]{1,0:T(8,128)(2,1)}, bf16[112,768]{1,0:T(8,128)(2,1)S(1)}, u32[]{:S(2)}, u32[]{:S(2)}) %collective-permute-start.3) | collective-permute-done | bytes 172064 | tf_op jit(solution)/shard_map/ppermute | solution.py:37
  22.1 2.9 %own_attention.1 = (bf16[4,576,512]{2,1,0:T(8,128)(2,1)S(1)}, bf16[4,192,512]{2,1,0:T(8,128)(2,1)S(1)}, f32[4,8,512]{2,1,0:T(8,128)S(1)}, bf16[4,576,768]{2,1,0:T(8,128)(2,1)S(1)}, bf16[4,192,768]{2,1,0:T(8,128)(2,1)S(1)}) custom-call(s32[3]{0:T(128)S(1)} %pad_add_fusion.places, bf16[512,768]{1,0:T(8,128)(2,1)S(1)} %constant_dynamic-slice_fusion.refs_0_.refs_2_, ...), custom_call_target="tpu_custom_call" | custom-call | flops 10066329600 | tf_op jit(solution)/shard_map/own_attention/pallas_call | solution.py:135
  27.7 3.4 %collective-permute-done.4.refs_1_.refs_3_ = bf16[112,768]{1,0:T(8,128)(2,1)S(1)} collective-permute-done((bf16[112,768]{1,0:T(8,128)(2,1)S(1)}, bf16[112,768]{1,0:T(8,128)(2,1)S(1)}, u32[]{:S(2)}, u32[]{:S(2)}) %collective-permute-start.4) | collective-permute-done | bytes 172064 | tf_op jit(solution)/shard_map/ppermute | solution.py:37
  36.4 3.5 %collective-permute-done.12.refs_2_ = bf16[2,96,768]{2,1,0:T(8,128)(2,1)S(1)} collective-permute-done((bf16[2,96,768]{2,1,0:T(8,128)(2,1)S(1)}, bf16[2,96,768]{2,1,0:T(8,128)(2,1)S(1)}, u32[]{:S(2)}, u32[]{:S(2)}) %collective-permute-start.12) | collective-permute-done | bytes 294944 | tf_op jit(solution)/shard_map/ppermute | solution.py:37
  40.0 3.4 %far_attention.3 = (bf16[4,576,512]{2,1,0:T(8,128)(2,1)S(1)}, bf16[4,192,512]{2,1,0:T(8,128)(2,1)S(1)}, f32[4,8,512]{2,1,0:T(8,128)S(1)}, bf16[4,576,768]{2,1,0:T(8,128)(2,1)S(1)}, bf16[4,192,768]{2,1,0:T(8,128)(2,1)S(1)}) custom-call(s32[3]{0:T(128)S(1)} %pad_add_fusion.places, ...), custom_call_target="tpu_custom_call", output_to_operand_aliasing={{0}: (8, {}), {1}: (9, {}), {2}: (10, {}), {3}: (11, {}), {... | custom-call | flops 125829120000 | tf_op jit(solution)/shard_map/far_attention/pallas_call | solution.py:135
  45.3 3.0 %far_attention.4 = (bf16[4,576,512]{2,1,0:T(8,128)(2,1)S(1)}, bf16[4,192,512]{2,1,0:T(8,128)(2,1)S(1)}, f32[4,8,512]{2,1,0:T(8,128)S(1)}, bf16[4,576,768]{2,1,0:T(8,128)(2,1)S(1)}, bf16[4,192,768]{2,1,0:T(8,128)(2,1)S(1)}) custom-call(s32[3]{0:T(128)S(1)} %pad_add_fusion.places, ...), custom_call_target="tpu_custom_call", output_to_operand_aliasing={{0}: (8, {}), {1}: (9, {}), {2}: (10, {}), {3}: (11, {}), {... | custom-call | flops 125829120000 | tf_op jit(solution)/shard_map/far_attention/pallas_call | solution.py:135
  48.5 3.7 %far_attention.5 = (bf16[4,576,512]{2,1,0:T(8,128)(2,1)S(1)}, bf16[4,192,512]{2,1,0:T(8,128)(2,1)S(1)}, f32[4,8,512]{2,1,0:T(8,128)S(1)}, bf16[4,576,768]{2,1,0:T(8,128)(2,1)S(1)}, bf16[4,192,768]{2,1,0:T(8,128)(2,1)S(1)}) custom-call(s32[3]{0:T(128)S(1)} %pad_add_fusion.places, ...), custom_call_target="tpu_custom_call", output_to_operand_aliasing={{0}: (8, {}), {1}: (9, {}), {2}: (10, {}), {3}: (11, {}), {... | custom-call | flops 125829120000 | tf_op jit(solution)/shard_map/far_attention/pallas_call | solution.py:135
  52.8 18.2 %feed_forward.1 = (bf16[4,512,384]{2,1,0:T(8,128)(2,1)S(1)}, bf16[4,512,384]{2,1,0:T(8,128)(2,1)S(1)}, bf16[4,512,384]{2,1,0:T(8,128)(2,1)S(1)}, bf16[4,512,768]...) custom-call(s32[3]{0:T(128)S(1)} %pad_add_fusion.places, ...), custom_call_target="tpu_custom_call" | custom-call | flops 38654705664 | tf_op jit(solution)/shard_map/feed_forward/pallas_call | solution.py:135
  71.5 3.8 %inner_back.1 = (bf16[4,512,384]{2,1,0:T(8,128)(2,1)S(1)}, bf16[4,512,384]{2,1,0:T(8,128)(2,1)S(1)}, f32[4,1,768]{2,1,0:T(1,128)S(1)}, f32[8,128]{1,0:T(8,128)S(1)}) custom-call(s32[3]{0:T(128)S(1)} %pad_add_fusion.places, bf16[4,512,384]{2,1,0:T(8,128)(2,1)S(1)} %get-tuple-element.132.refs_0_.refs_2_, bf16[3072,768]{1,0:T(8,128)(2,1)S(1)} %copy-done.4, ...), custom_call_target="tpu_custom_call" | custom-call | flops 19327352832 | tf_op jit(solution)/shard_map/inner_back/pallas_call | solution.py:135
  76.7 3.2 %down_grad.1 = (bf16[2,768,384]{2,1,0:T(8,128)(2,1)S(1)}, bf16[2,768,384]{2,1,0:T(8,128)(2,1)S(1)}, f32[8,128]{1,0:T(8,128)S(1)}) custom-call(s32[3]{0:T(128)S(1)} %pad_add_fusion.places, bf16[4,512,384]{2,1,0:T(8,128)(2,1)S(1)} %get-tuple-element.140.refs_0_, bf16[4,512,384]{2,1,0:T(8,128)(2,1)S(1)} %collective-permute-done.18.refs_1_, ...), custom_call_target="tpu_custom_call" | custom-call | flops 19327352832 | tf_op jit(solution)/shard_map/down_grad/pallas_call | solution.py:135
  79.9 3.2 %up_grad.1 = (bf16[4,192,384]{2,1,0:T(8,128)(2,1)S(1)}, bf16[4,192,384]{2,1,0:T(8,128)(2,1)S(1)}, bf16[4,192,384]{2,1,0:T(8,128)(2,1)S(1)}, bf16[4,192,384]{2,1,0:T(8,128)(2,1)S(1)}, f32[8,128]{1,0:T(8,128)S(1)}) custom-call(s32[3]{0:T(128)S(1)} %pad_add_fusion.places, bf16[4,512,384]{2,1,0:T(8,128)(2,1)S(1)} %get-tuple-element.135.refs_0_, ...), custom_call_target="tpu_custom_call" | custom-call | flops 24159192 | tf_op jit(solution)/shard_map/up_grad/pallas_call | solution.py:135
  86.1 4.3 %hidden_back.1 = (bf16[512,384]{1,0:T(8,128)(2,1)S(1)}, f32[512,768]{1,0:T(8,128)S(1)}, bf16[512,768]{1,0:T(8,128)(2,1)S(1)}, f32[8,768]{1,0:T(8,128)S(1)}, f32[8,128]{1,0:T(8,128)S(1)}) custom-call(s32[3]{0:T(128)S(1)} %pad_add_fusion.places, bf16[4,512,384]{2,1,0:T(8,128)(2,1)S(1)} %get-tuple-element.135.refs_0_, ...), custom_call_target="tpu_custom_call" | custom-call | flops 24159192 | tf_op jit(solution)/shard_map/hidden_back/pallas_call | solution.py:135
  90.4 11.9 %attention_back.1 = (bf16[4,576,512]{2,1,0:T(8,128)(2,1)S(1)}, f32[4,8,576]{2,1,0:T(8,128)S(1)}, f32[8,128]{1,0:T(8,128)S(1)}) custom-call(s32[3]{0:T(128)S(1)} %pad_add_fusion.places, bf16[4,576,512]{2,1,0:T(8,128)(2,1)S(1)} %get-tuple-element.131.refs_0_, bf16[4,192,768]{2,1,0:T(8,128)(2,1)S(1)} %get-tuple-element.129.refs_2_.refs_1_, ...), custom_call_target="tpu_custom_call" | custom-call | tf_op jit(solution)/shard_map/attention_back/pallas_call | solution.py:135
  102.4 3.7 %input_sum.1 = (f32[512,768]{1,0:T(8,128)}, f32[8,128]{1,0:T(8,128)S(1)}) custom-call(s32[3]{0:T(128)S(1)} %pad_add_fusion.places, bf16[4,576,512]{2,1,0:T(8,128)(2,1)S(1)} %get-tuple-element.148.refs_0_, bf16[4,576,768]{2,1,0:T(8,128)(2,1)S(1)} %get-tuple-element.149.refs_1_, f32[512,768]{1,0:T(8,128)S(1)} %get-tuple-element.150.refs_2_, ...), custom_call_target="tpu_custom_call" | custom-call | bytes 90439 | tf_op jit(solution)/shard_map/input_sum/pallas_call | solution.py:92
  113.6 4.0 %attn_grad.1 = (bf16[4,192,384]{2,1,0:T(8,128)(2,1)S(1)}, bf16[4,192,384]{2,1,0:T(8,128)(2,1)S(1)}, bf16[4,224,384]{2,1,0:T(8,128)(2,1)S(1)}, bf16[4,224,384]{2,1,0:T(8,128)(2,1)S(1)}, f32[8,128]{1,0:T(8,128)S(1)}) custom-call(s32[3]{0:T(128)S(1)} %pad_add_fusion.places, bf16[4,576,512]{2,1,0:T(8,128)(2,1)S(1)} %get-tuple-element.148.refs_0_, ...), custom_call_target="tpu_custom_call" | custom-call | tf_op jit(solution)/shard_map/attn_grad/pallas_call | solution.py:135
  119.8 5.8 %collective-permute-done.27.refs_1_ = bf16[768,384]{1,0:T(8,128)(2,1)S(1)} collective-permute-done((bf16[768,384]{1,0:T(8,128)(2,1)S(1)}, bf16[768,384]{1,0:T(8,128)(2,1)S(1)}, u32[]{:S(2)}, u32[]{:S(2)}) %collective-permute-start.27) | collective-permute-done | bytes 589856 | tf_op jit(solution)/shard_map/ppermute | solution.py:37
  130.0 8.2 %collective-permute-done.25.refs_1_ = bf16[4,192,384]{2,1,0:T(8,128)(2,1)S(1)} collective-permute-done((bf16[4,192,384]{2,1,0:T(8,128)(2,1)S(1)}, bf16[4,192,384]{2,1,0:T(8,128)(2,1)S(1)}, u32[]{:S(2)}, u32[]{:S(2)}) %collective-permute-start.25) | collective-permute-done | bytes 589856 | tf_op jit(solution)/shard_map/ppermute | solution.py:37
  138.2 3.3 %collective-permute-done.26.refs_3_ = bf16[4,224,384]{2,1,0:T(8,128)(2,1)S(1)} collective-permute-done((bf16[4,224,384]{2,1,0:T(8,128)(2,1)S(1)}, bf16[4,224,384]{2,1,0:T(8,128)(2,1)S(1)}, u32[]{:S(2)}, u32[]{:S(2)}) %collective-permute-start.26) | collective-permute-done | bytes 688160 | tf_op jit(solution)/shard_map/ppermute | solution.py:37
  151.9 6.4 %collective-permute-done.35.refs_1_ = bf16[384,384]{1,0:T(8,128)(2,1)S(1)} collective-permute-done((bf16[384,384]{1,0:T(8,128)(2,1)S(1)}, bf16[384,384]{1,0:T(8,128)(2,1)S(1)}, u32[]{:S(2)}, u32[]{:S(2)}) %collective-permute-start.35) | collective-permute-done | bytes 294944 | tf_op jit(solution)/shard_map/ppermute | solution.py:37
  165.6 4.9 %collective-permute-done.36.refs_1_ = bf16[208,384]{1,0:T(8,128)(2,1)S(1)} collective-permute-done((bf16[208,384]{1,0:T(8,128)(2,1)S(1)}, bf16[208,384]{1,0:T(8,128)(2,1)S(1)}, u32[]{:S(2)}, u32[]{:S(2)}) %collective-permute-start.36) | collective-permute-done | bytes 159776 | tf_op jit(solution)/shard_map/ppermute | solution.py:37
  174.6 2.8 %collective-permute-done.41.refs_2_ = bf16[384,384]{1,0:T(8,128)(2,1)S(1)} collective-permute-done((bf16[384,384]{1,0:T(8,128)(2,1)S(1)}, bf16[384,384]{1,0:T(8,128)(2,1)S(1)}, u32[]{:S(2)}, u32[]{:S(2)}) %collective-permute-start.41) | collective-permute-done | bytes 294944 | tf_op jit(solution)/shard_map/ppermute | solution.py:37
  181.8 3.8 %ffn_place.1 = (f32[768,768]{1,0:T(8,128)}, f32[768,768]{1,0:T(8,128)}, f32[8,128]{1,0:T(8,128)S(1)}) custom-call(s32[3]{0:T(128)S(1)} %pad_add_fusion.places, bf16[4,384,384]{2,1,0:T(8,128)(2,1)S(1)} %get-tuple-element.203.refs_0_, bf16[4,384,384]{2,1,0:T(8,128)(2,1)S(1)} %collective-permute-done.44.refs_1_, f32[8,128]{1,0:T(8,128)S(1)} %get-tuple-element.204.refs_2_), custom_call_target="tpu_custom_call" | custom-call | bytes 56623104 | tf_op jit(solution)/shard_map/ffn_place/pallas_call | solution.py:92
  (132 shorter events, 68.7 us)
Async XLA Ops:
  3.3 10.4 %collective-permute-start.2 = (bf16[112,768]{1,0:T(8,128)(2,1)}, bf16[112,768]{1,0:T(8,128)(2,1)}, u32[]{:S(2)}, u32[]{:S(2)}) collective-permute-start(bf16[112,768]{1,0:T(8,128)(2,1)} %pad_maximum_fusion.1), channel_id=1, source_target_pairs={{0,1},{1,0},{2,3},{3,2},{4,5},{5,4},{6,7},{7,6},{8,9},{9,8},{10,11... | collective-permute-start | bytes 516104 | tf_op jit(solution)/shard_map/ppermute | solution.py:37
  6.3 18.7 %collective-permute-start.1 = (bf16[112,768]{1,0:T(8,128)(2,1)}, bf16[112,768]{1,0:T(8,128)(2,1)S(1)}, u32[]{:S(2)}, u32[]{:S(2)}) collective-permute-start(bf16[112,768]{1,0:T(8,128)(2,1)} %pad_maximum_fusion.1), channel_id=1, source_target_pairs={{0,2},{1,3},{2,0},{3,1},{4,6},{5,7},{6,4},{7,5},{8,10},{9,11},{10,... | collective-permute-start | bytes 516104 | tf_op jit(solution)/shard_map/ppermute | solution.py:37
  8.9 16.1 %collective-permute-start = (bf16[112,768]{1,0:T(8,128)(2,1)}, bf16[112,768]{1,0:T(8,128)(2,1)S(1)}, u32[]{:S(2)}, u32[]{:S(2)}) collective-permute-start(bf16[112,768]{1,0:T(8,128)(2,1)} %pad_maximum_fusion.1), channel_id=1, source_target_pairs={{0,3},{1,2},{2,1},{3,0},{4,7},{5,6},{6,5},{7,4},{8,11},{9,10},{10,... | collective-permute-start | bytes 516104 | tf_op jit(solution)/shard_map/ppermute | solution.py:37
  20.3 13.5 %collective-permute-start.8 = (bf16[2,96,768]{2,1,0:T(8,128)(2,1)S(1)}, bf16[2,96,768]{2,1,0:T(8,128)(2,1)S(1)}, u32[]{:S(2)}, u32[]{:S(2)}) collective-permute-start(bf16[2,96,768]{2,1,0:T(8,128)(2,1)S(1)} %pair_rows.3.refs_4_.refs_1_), channel_id=1, source_target_pairs={{0,16},{8,24},{16,0},{24,8},{1,17},{9,25},{17,1},{25,9},{2,18},{10... | collective-permute-start | bytes 884744 | tf_op jit(solution)/shard_map/ppermute | solution.py:37
  35.0 13.3 %collective-permute-start.7 = (bf16[2,96,768]{2,1,0:T(8,128)(2,1)}, bf16[2,96,768]{2,1,0:T(8,128)(2,1)}, u32[]{:S(2)}, u32[]{:S(2)}) collective-permute-start(bf16[2,96,768]{2,1,0:T(8,128)(2,1)} %pair_rows.4.refs_1_), channel_id=1, source_target_pairs={{0,4},{4,0},{1,5},{5,1},{2,6},{6,2},{3,7},{7,3},{8,12},{12,8},{9,1... | collective-permute-start | bytes 884744 | tf_op jit(solution)/shard_map/ppermute | solution.py:37
  35.5 9.1 %collective-permute-start.6 = (bf16[2,96,768]{2,1,0:T(8,128)(2,1)}, bf16[2,96,768]{2,1,0:T(8,128)(2,1)S(1)}, u32[]{:S(2)}, u32[]{:S(2)}) collective-permute-start(bf16[2,96,768]{2,1,0:T(8,128)(2,1)} %pair_rows.4.refs_1_), channel_id=1, source_target_pairs={{0,16},{8,24},{16,0},{24,8},{1,17},{9,25},{17,1},{25,9},{2,18},{10... | collective-permute-start | bytes 884744 | tf_op jit(solution)/shard_map/ppermute | solution.py:37
  36.4 8.9 %collective-permute-start.13 = (bf16[2,96,768]{2,1,0:T(8,128)(2,1)S(1)}, bf16[2,96,768]{2,1,0:T(8,128)(2,1)S(1)}, u32[]{:S(2)}, u32[]{:S(2)}) collective-permute-start(bf16[2,96,768]{2,1,0:T(8,128)(2,1)S(1)} %pair_rows.5.refs_1_), channel_id=1, source_target_pairs={{0,4},{4,0},{1,5},{5,1},{2,6},{6,2},{3,7},{7,3},{8,12},{12,8},{9,1... | collective-permute-start | bytes 884744 | tf_op jit(solution)/shard_map/ppermute | solution.py:37
  52.2 19.4 %collective-permute-start.15 = (bf16[4,192,512]{2,1,0:T(8,128)(2,1)S(1)}, bf16[4,192,512]{2,1,0:T(8,128)(2,1)S(1)}, u32[]{:S(2)}, u32[]{:S(2)}) collective-permute-start(bf16[4,192,512]{2,1,0:T(8,128)(2,1)S(1)} %get-tuple-element.128.refs_1_.refs_4_), channel_id=1, source_target_pairs={{0,4},{4,0},{1,5},{5,1},{2,6},{6,2},{3,7},{7,3},{8,12},{12,8},{9,1... | collective-permute-start | bytes 2359304 | tf_op jit(solution)/shard_map/ppermute | solution.py:37
  79.9 28.1 %collective-permute-start.22 = (bf16[2,768,384]{2,1,0:T(8,128)(2,1)S(1)}, bf16[2,768,384]{2,1,0:T(8,128)(2,1)S(1)}, u32[]{:S(2)}, u32[]{:S(2)}) collective-permute-start(bf16[2,768,384]{2,1,0:T(8,128)(2,1)S(1)} %get-tuple-element.160), channel_id=1, source_target_pairs={{0,1},{1,0},{2,3},{3,2},{4,5},{5,4},{6,7},{7,6},{8,9},{9,8},{10,11... | collective-permute-start | bytes 3538952 | tf_op jit(solution)/shard_map/ppermute | solution.py:37
  83.1 24.9 %collective-permute-start.23 = (bf16[4,192,384]{2,1,0:T(8,128)(2,1)S(1)}, bf16[4,192,384]{2,1,0:T(8,128)(2,1)S(1)}, u32[]{:S(2)}, u32[]{:S(2)}) collective-permute-start(bf16[4,192,384]{2,1,0:T(8,128)(2,1)S(1)} %get-tuple-element.162), channel_id=1, source_target_pairs={{0,8},{8,0},{16,24},{24,16},{1,9},{9,1},{17,25},{25,17},{2,10},{10... | collective-permute-start | bytes 1769480 | tf_op jit(solution)/shard_map/ppermute | solution.py:37
  84.7 23.3 %collective-permute-start.24 = (bf16[4,192,384]{2,1,0:T(8,128)(2,1)S(1)}, bf16[4,192,384]{2,1,0:T(8,128)(2,1)S(1)}, u32[]{:S(2)}, u32[]{:S(2)}) collective-permute-start(bf16[4,192,384]{2,1,0:T(8,128)(2,1)S(1)} %get-tuple-element.164), channel_id=1, source_target_pairs={{0,16},{8,24},{16,0},{24,8},{1,17},{9,25},{17,1},{25,9},{2,18},{10... | collective-permute-start | bytes 1769480 | tf_op jit(solution)/shard_map/ppermute | solution.py:37
  102.3 11.3 %collective-permute-start.19 = (bf16[4,576,512]{2,1,0:T(8,128)(2,1)S(1)}, bf16[4,576,512]{2,1,0:T(8,128)(2,1)S(1)}, u32[]{:S(2)}, u32[]{:S(2)}) collective-permute-start(bf16[4,576,512]{2,1,0:T(8,128)(2,1)S(1)} %get-tuple-element.148.refs_0_), channel_id=1, source_target_pairs={{0,4},{4,0},{1,5},{5,1},{2,6},{6,2},{3,7},{7,3},{8,12},{12,8},{9,1... | collective-permute-start | bytes 7077896 | tf_op jit(solution)/shard_map/ppermute | solution.py:37
  109.3 16.3 %collective-permute-start.27 = (bf16[768,384]{1,0:T(8,128)(2,1)S(1)}, bf16[768,384]{1,0:T(8,128)(2,1)S(1)}, u32[]{:S(2)}, u32[]{:S(2)}) collective-permute-start(bf16[768,384]{1,0:T(8,128)(2,1)S(1)} %get-tuple-element.172), channel_id=1, source_target_pairs={{0,8},{8,0},{16,24},{24,16},{1,9},{9,1},{17,25},{25,17},{2,10},{10... | collective-permute-start | bytes 1769480 | tf_op jit(solution)/shard_map/ppermute | solution.py:37
  110.9 16.3 %collective-permute-start.28 = (bf16[768,384]{1,0:T(8,128)(2,1)S(1)}, bf16[768,384]{1,0:T(8,128)(2,1)S(1)}, u32[]{:S(2)}, u32[]{:S(2)}) collective-permute-start(bf16[768,384]{1,0:T(8,128)(2,1)S(1)} %get-tuple-element.174), channel_id=1, source_target_pairs={{0,16},{8,24},{16,0},{24,8},{1,17},{9,25},{17,1},{25,9},{2,18},{10... | collective-permute-start | bytes 1769480 | tf_op jit(solution)/shard_map/ppermute | solution.py:37
  117.7 20.5 %collective-permute-start.25 = (bf16[4,192,384]{2,1,0:T(8,128)(2,1)S(1)}, bf16[4,192,384]{2,1,0:T(8,128)(2,1)S(1)}, u32[]{:S(2)}, u32[]{:S(2)}) collective-permute-start(bf16[4,192,384]{2,1,0:T(8,128)(2,1)S(1)} %get-tuple-element.168), channel_id=1, source_target_pairs={{0,8},{8,0},{16,24},{24,16},{1,9},{9,1},{17,25},{25,17},{2,10},{10... | collective-permute-start | bytes 1769480 | tf_op jit(solution)/shard_map/ppermute | solution.py:37
  118.6 22.9 %collective-permute-start.26 = (bf16[4,224,384]{2,1,0:T(8,128)(2,1)S(1)}, bf16[4,224,384]{2,1,0:T(8,128)(2,1)S(1)}, u32[]{:S(2)}, u32[]{:S(2)}) collective-permute-start(bf16[4,224,384]{2,1,0:T(8,128)(2,1)S(1)} %get-tuple-element.170), channel_id=1, source_target_pairs={{0,16},{8,24},{16,0},{24,8},{1,17},{9,25},{17,1},{25,9},{2,18},{10... | collective-permute-start | bytes 2064392 | tf_op jit(solution)/shard_map/ppermute | solution.py:37
  128.0 16.4 %collective-permute-start.33 = (bf16[2,192,384]{2,1,0:T(8,128)(2,1)S(1)}, bf16[2,192,384]{2,1,0:T(8,128)(2,1)S(1)}, u32[]{:S(2)}, u32[]{:S(2)}) collective-permute-start(bf16[2,192,384]{2,1,0:T(8,128)(2,1)S(1)} %get-tuple-element.186), channel_id=1, source_target_pairs={{0,1},{1,0},{2,3},{3,2},{4,5},{5,4},{6,7},{7,6},{8,9},{9,8},{10,11... | collective-permute-start | bytes 884744 | tf_op jit(solution)/shard_map/ppermute | solution.py:37
  128.3 15.6 %collective-permute-start.31 = (bf16[2,96,384]{2,1,0:T(8,128)(2,1)S(1)}, bf16[2,96,384]{2,1,0:T(8,128)(2,1)S(1)}, u32[]{:S(2)}, u32[]{:S(2)}) collective-permute-start(bf16[2,96,384]{2,1,0:T(8,128)(2,1)S(1)} %get-tuple-element.182), channel_id=1, source_target_pairs={{0,8},{8,0},{16,24},{24,16},{1,9},{9,1},{17,25},{25,17},{2,10},{10... | collective-permute-start | bytes 442376 | tf_op jit(solution)/shard_map/ppermute | solution.py:37
  128.9 15.5 %collective-permute-start.32 = (bf16[2,96,384]{2,1,0:T(8,128)(2,1)S(1)}, bf16[2,96,384]{2,1,0:T(8,128)(2,1)S(1)}, u32[]{:S(2)}, u32[]{:S(2)}) collective-permute-start(bf16[2,96,384]{2,1,0:T(8,128)(2,1)S(1)} %get-tuple-element.184), channel_id=1, source_target_pairs={{0,16},{8,24},{16,0},{24,8},{1,17},{9,25},{17,1},{25,9},{2,18},{10... | collective-permute-start | bytes 442376 | tf_op jit(solution)/shard_map/ppermute | solution.py:37
  145.1 13.2 %collective-permute-start.35 = (bf16[384,384]{1,0:T(8,128)(2,1)S(1)}, bf16[384,384]{1,0:T(8,128)(2,1)S(1)}, u32[]{:S(2)}, u32[]{:S(2)}) collective-permute-start(bf16[384,384]{1,0:T(8,128)(2,1)S(1)} %get-tuple-element.192), channel_id=1, source_target_pairs={{0,2},{1,3},{2,0},{3,1},{4,6},{5,7},{6,4},{7,5},{8,10},{9,11},{10,... | collective-permute-start | bytes 884744 | tf_op jit(solution)/shard_map/ppermute | solution.py:37
  151.0 10.9 %collective-permute-start.34 = (bf16[2,208,384]{2,1,0:T(8,128)(2,1)S(1)}, bf16[2,208,384]{2,1,0:T(8,128)(2,1)S(1)}, u32[]{:S(2)}, u32[]{:S(2)}) collective-permute-start(bf16[2,208,384]{2,1,0:T(8,128)(2,1)S(1)} %get-tuple-element.190), channel_id=1, source_target_pairs={{0,1},{1,0},{2,3},{3,2},{4,5},{5,4},{6,7},{7,6},{8,9},{9,8},{10,11... | collective-permute-start | bytes 958472 | tf_op jit(solution)/shard_map/ppermute | solution.py:37
  159.0 14.2 %collective-permute-start.42 = (bf16[384,384]{1,0:T(8,128)(2,1)S(1)}, bf16[384,384]{1,0:T(8,128)(2,1)S(1)}, u32[]{:S(2)}, u32[]{:S(2)}) collective-permute-start(bf16[384,384]{1,0:T(8,128)(2,1)S(1)} %get-tuple-element.199.refs_0_), channel_id=1, source_target_pairs={{0,24},{8,16},{16,8},{24,0},{1,25},{9,17},{17,9},{25,1},{2,26},{10... | collective-permute-start | bytes 884744 | tf_op jit(solution)/shard_map/ppermute | solution.py:37
  164.0 13.4 %collective-permute-start.41 = (bf16[384,384]{1,0:T(8,128)(2,1)S(1)}, bf16[384,384]{1,0:T(8,128)(2,1)S(1)}, u32[]{:S(2)}, u32[]{:S(2)}) collective-permute-start(bf16[384,384]{1,0:T(8,128)(2,1)S(1)} %get-tuple-element.199.refs_0_), channel_id=1, source_target_pairs={{0,16},{8,24},{16,0},{24,8},{1,17},{9,25},{17,1},{25,9},{2,18},{10... | collective-permute-start | bytes 884744 | tf_op jit(solution)/shard_map/ppermute | solution.py:37
  164.5 12.9 %collective-permute-start.40 = (bf16[384,384]{1,0:T(8,128)(2,1)S(1)}, bf16[384,384]{1,0:T(8,128)(2,1)S(1)}, u32[]{:S(2)}, u32[]{:S(2)}) collective-permute-start(bf16[384,384]{1,0:T(8,128)(2,1)S(1)} %get-tuple-element.199.refs_0_), channel_id=1, source_target_pairs={{0,8},{8,0},{16,24},{24,16},{1,9},{9,1},{17,25},{25,17},{2,10},{10... | collective-permute-start | bytes 884744 | tf_op jit(solution)/shard_map/ppermute | solution.py:37
  (35 other events, 192.4 us)
